TPU v7x, 32 devices: a whole 2x2x4 slice. The times are simulated.
32 devices in a mesh: tile: 8 (over z, y), batch: 4 (over x, core).
Axes of the slice: x: 2, y: 2, z: 4, core: 2. Of those that a mesh axis runs over, the one named last changes fastest.
Arguments:
- states: bfloat16 [4, 64, 16, 16, 256], P('batch', 'tile'), may hold values from -6 to 6
- cotangent: bfloat16 [4, 64, 16, 16, 256], P('batch', 'tile'), may hold values from -6 to 6
- beside_slot: int32 [64, 8], replicated, may hold values from 0 to 63, as said below
- beside_code: int32 [64, 8], replicated, may hold values from 0 to 7
- mixers: bfloat16 [2, 256, 256], replicated, may hold values from -0.375 to 0.375
- stencils: float32 [2, 9, 256], replicated, may hold values from -2 to 2
- shifts: float32 [2, 256], replicated, may hold values from -3 to 3
Outputs:
- outcome: bfloat16 [4, 64, 16, 16, 256], P('batch', 'tile')
- state_grad: bfloat16 [4, 64, 16, 16, 256], P('batch', 'tile')
- mixer_grads: float32 [2, 256, 256], replicated
- stencil_grads: float32 [2, 9, 256], replicated
- shift_grads: float32 [2, 256], replicated
Inputs may be any that keep to these rules, and one draw needn't show every extreme that they name: `beside_slot`: tiles are numbered by slot; the tiles of one aligned block of 8 slots have 8 * 8 entries, of which at most 2 name slots of any one other block, and in every block exactly 2 entries name one other block; how many entries of a block name other blocks varies from block to block.
All inputs are finite; a program needn't handle non-finite values.
Results may differ from a plain program's by a relative error of at most 0.009.
Values may be sent and summed in bfloat16 or wider, within the bound.
A program may use at most 128 MiB of HBM per device.

v0:
```python
import math

import jax
import jax.numpy as jnp
from jax import lax
from jax.sharding import PartitionSpec as P

CAP = 2


SQRT_HALF = 0.7071067811865476
INV_ROOT_TAU = 0.3989422804014327


def gelu_exact(value):
    return 0.5 * value * (1.0 + lax.erf(value * SQRT_HALF))


def gelu_slope(value):
    return (
        0.5 * (1.0 + lax.erf(value * SQRT_HALF))
        + value * jnp.exp(-0.5 * value * value) * INV_ROOT_TAU
    )


def rim_rows(field):
    return jnp.stack(
        [field[:, :, 0], field[:, :, :, -1], field[:, :, -1], field[:, :, :, 0]], axis=2
    )


def assemble(field, panels, flip_bits):
    turned = jnp.where(flip_bits[None, :, :, None, None] == 1, panels[:, :, :, ::-1], panels)
    corners = turned[:, :, 4:, 0]
    top_row = jnp.concatenate([corners[:, :, 3:4], turned[:, :, 0], corners[:, :, 0:1]], axis=2)
    bottom = jnp.concatenate([corners[:, :, 2:3], turned[:, :, 2], corners[:, :, 1:2]], axis=2)
    middle = jnp.concatenate(
        [turned[:, :, 3][:, :, :, None], field, turned[:, :, 1][:, :, :, None]], axis=3
    )
    return jnp.concatenate([top_row[:, :, None], middle, bottom[:, :, None]], axis=2)


def stencil_apply(padded, kernel):
    side_len = padded.shape[2] - 2
    running = jnp.zeros(padded.shape[:2] + (side_len, side_len, padded.shape[4]), jnp.float32)
    for row_at in range(3):
        for col_at in range(3):
            window = padded[:, :, row_at : row_at + side_len, col_at : col_at + side_len]
            running = running + kernel[3 * row_at + col_at] * window.astype(jnp.float32)
    return running


def stencil_back(grad, kernel):
    widened = grad.astype(jnp.float32)
    running = jnp.zeros(
        grad.shape[:2] + (grad.shape[2] + 2, grad.shape[3] + 2, grad.shape[4]), jnp.float32
    )
    for row_at in range(3):
        for col_at in range(3):
            running = running + jnp.pad(
                kernel[3 * row_at + col_at] * widened,
                ((0, 0), (0, 0), (row_at, 2 - row_at), (col_at, 2 - col_at), (0, 0)),
            )
    return running


def stencil_grad(grad, padded):
    side_len = grad.shape[2]
    widened = grad.astype(jnp.float32)
    terms = []
    for row_at in range(3):
        for col_at in range(3):
            window = padded[:, :, row_at : row_at + side_len, col_at : col_at + side_len].astype(
                jnp.float32
            )
            terms.append(jnp.sum(widened * window, axis=(0, 1, 2, 3)))
    return jnp.stack(terms)


def halo_parts(padded_grad, flip_bits):
    side_len = padded_grad.shape[2] - 2
    side_parts = jnp.stack(
        [
            padded_grad[:, :, 0, 1:-1],
            padded_grad[:, :, 1:-1, -1],
            padded_grad[:, :, -1, 1:-1],
            padded_grad[:, :, 1:-1, 0],
        ],
        axis=2,
    )
    corner_vals = jnp.stack(
        [
            padded_grad[:, :, 0, -1],
            padded_grad[:, :, -1, -1],
            padded_grad[:, :, -1, 0],
            padded_grad[:, :, 0, 0],
        ],
        axis=2,
    )
    flip_wide = flip_bits[None, :, :, None, None]
    side_parts = jnp.where(flip_wide[:, :, :4] == 1, side_parts[:, :, :, ::-1], side_parts)
    positions = jnp.arange(side_len)
    first_spot = (positions == 0).astype(jnp.float32)[:, None]
    last_spot = (positions == side_len - 1).astype(jnp.float32)[:, None]
    corner_spot = jnp.where(flip_wide[:, :, 4:] == 1, last_spot, first_spot)
    return jnp.concatenate([side_parts, corner_spot * corner_vals[:, :, :, None]], axis=2)


def add_rims(inner, rim_grad):
    inner = inner.at[:, :, 0].add(rim_grad[:, :, 0])
    inner = inner.at[:, :, :, -1].add(rim_grad[:, :, 1])
    inner = inner.at[:, :, -1].add(rim_grad[:, :, 2])
    inner = inner.at[:, :, :, 0].add(rim_grad[:, :, 3])
    return inner


def block_pass(
    states, cotangent, panel_fetch, send_back, flip_bits, mixers, stencils, shifts, early
):
    shape = states.shape
    channels = shape[4]
    padded_in = assemble(states, panel_fetch(states), flip_bits)
    conv_first = stencil_apply(padded_in, stencils[0]).astype(jnp.bfloat16)
    flat_first = conv_first.reshape(-1, channels)
    hidden = jnp.dot(flat_first, mixers[0], preferred_element_type=jnp.float32) + shifts[0]
    active = gelu_exact(hidden).astype(jnp.bfloat16).reshape(shape)
    padded_mid = assemble(active, panel_fetch(active), flip_bits)
    conv_second = stencil_apply(padded_mid, stencils[1]).astype(jnp.bfloat16)
    flat_second = conv_second.reshape(-1, channels)
    outcome = (
        states.reshape(-1, channels).astype(jnp.float32)
        + jnp.dot(flat_second, mixers[1], preferred_element_type=jnp.float32)
        + shifts[1]
    ).astype(jnp.bfloat16)
    upstream = cotangent.reshape(-1, channels)
    mixer_second = lax.dot_general(
        flat_second, upstream, (((0,), (0,)), ((), ())), preferred_element_type=jnp.float32
    )
    shift_second = jnp.sum(upstream.astype(jnp.float32), axis=0)
    grad_second = (
        lax.dot_general(
            upstream, mixers[1], (((1,), (1,)), ((), ())), preferred_element_type=jnp.float32
        )
        .astype(jnp.bfloat16)
        .reshape(shape)
    )
    stencil_second = stencil_grad(grad_second, padded_mid)
    later = early((mixer_second, stencil_second, shift_second))
    grad_active = send_back(stencil_back(grad_second, stencils[1]))
    grad_hidden = (grad_active.reshape(-1, channels) * gelu_slope(hidden)).astype(jnp.bfloat16)
    mixer_first = lax.dot_general(
        flat_first, grad_hidden, (((0,), (0,)), ((), ())), preferred_element_type=jnp.float32
    )
    shift_first = jnp.sum(grad_hidden.astype(jnp.float32), axis=0)
    grad_conv = (
        lax.dot_general(
            grad_hidden, mixers[0], (((1,), (1,)), ((), ())), preferred_element_type=jnp.float32
        )
        .astype(jnp.bfloat16)
        .reshape(shape)
    )
    stencil_first = stencil_grad(grad_conv, padded_in)
    state_grad = (
        cotangent.astype(jnp.float32) + send_back(stencil_back(grad_conv, stencils[0]))
    ).astype(jnp.bfloat16)
    return (outcome.reshape(shape), state_grad, (mixer_first, stencil_first, shift_first), later)


def shards(states, cotangent, beside_slot, beside_code, mixers, stencils, shifts):
    samples = states.shape[0]
    tile_count = states.shape[1]
    side_len = states.shape[2]
    channels = states.shape[4]
    groups = lax.axis_size("tile")
    own_index = lax.axis_index("tile")
    entries = tile_count * 8
    owner_all = (beside_slot // tile_count).reshape(groups, entries)
    source_all = (beside_slot % tile_count * 4 + beside_code // 2).reshape(groups, entries)
    peer_ids = jnp.arange(groups, dtype=jnp.int32)
    entry_ids = jnp.arange(entries, dtype=jnp.int32)
    remote_all = owner_all != peer_ids[:, None]
    earlier = (owner_all[:, :, None] == owner_all[:, None, :]) & (
        entry_ids[None, None, :] < entry_ids[None, :, None]
    )
    place_all = jnp.sum(earlier.astype(jnp.int32), axis=2)
    wanted = remote_all & (owner_all == own_index)
    slot_ids = jnp.arange(CAP, dtype=jnp.int32)
    chosen = wanted[:, None, :] & (place_all[:, None, :] == slot_ids[None, :, None])
    send_rim = jnp.sum(jnp.where(chosen, source_all[:, None, :], 0), axis=2).reshape(-1)
    send_live = jnp.any(chosen, axis=2).reshape(-1)
    own_owner = lax.dynamic_index_in_dim(owner_all, own_index, 0, keepdims=False)
    own_place = lax.dynamic_index_in_dim(place_all, own_index, 0, keepdims=False)
    own_source = lax.dynamic_index_in_dim(source_all, own_index, 0, keepdims=False)
    own_remote = own_owner != own_index
    from_peer = jnp.where(own_remote, own_owner * CAP + own_place, 0)
    flip_bits = lax.dynamic_slice_in_dim(beside_code % 2, own_index * tile_count, tile_count, 0)
    mail_ids = jnp.arange(groups * CAP, dtype=jnp.int32)
    mail_match = own_remote[None, :] & (from_peer[None, :] == mail_ids[:, None])
    mail_entry = jnp.sum(jnp.where(mail_match, entry_ids[None, :], 0), axis=1)
    mail_live = jnp.any(mail_match, axis=1)

    def panel_fetch(field):
        rims = rim_rows(field).reshape(samples, tile_count * 4, side_len, channels)
        outgoing = jnp.where(
            send_live[None, :, None, None],
            jnp.take(rims, send_rim, axis=1),
            jnp.zeros((), jnp.bfloat16),
        )
        incoming = lax.all_to_all(
            outgoing.reshape(samples, groups, CAP, side_len, channels),
            "tile",
            split_axis=1,
            concat_axis=1,
            tiled=True,
        )
        incoming = incoming.reshape(samples, groups * CAP, side_len, channels)
        panels = jnp.where(
            own_remote[None, :, None, None],
            jnp.take(incoming, from_peer, axis=1),
            jnp.take(rims, own_source, axis=1),
        )
        return panels.reshape(samples, tile_count, 8, side_len, channels)

    def send_back(padded_grad):
        parts = halo_parts(padded_grad, flip_bits).reshape(samples, entries, side_len, channels)
        outgoing = jnp.where(
            mail_live[None, :, None, None],
            jnp.take(parts, mail_entry, axis=1),
            jnp.zeros((), jnp.float32),
        )
        incoming = lax.all_to_all(
            outgoing.reshape(samples, groups, CAP, side_len, channels),
            "tile",
            split_axis=1,
            concat_axis=1,
            tiled=True,
        )
        incoming = incoming.reshape(samples, groups * CAP, side_len, channels)
        kept_parts = jnp.where(own_remote[None, :, None, None], jnp.zeros((), jnp.float32), parts)
        returned = jnp.where(send_live[None, :, None, None], incoming, jnp.zeros((), jnp.float32))
        rim_grad = jnp.zeros((samples, tile_count * 4, side_len, channels), jnp.float32)
        rim_grad = rim_grad.at[:, own_source].add(kept_parts)
        rim_grad = rim_grad.at[:, send_rim].add(returned)
        return add_rims(
            padded_grad[:, :, 1:-1, 1:-1],
            rim_grad.reshape(samples, tile_count, 4, side_len, channels),
        )

    def early(group):
        return group

    outcome, state_grad, first, second = block_pass(
        states, cotangent, panel_fetch, send_back, flip_bits, mixers, stencils, shifts, early
    )
    summed = lax.psum(
        (first[0], first[1], first[2], second[0], second[1], second[2]), ("tile", "batch")
    )
    first = summed[:3]
    second = summed[3:]
    scale = 1.0 / math.sqrt(
        samples * tile_count * side_len * side_len * groups * lax.axis_size("batch")
    )
    mixer_grads = jnp.stack([first[0], second[0]]) * scale
    stencil_grads = jnp.stack([first[1], second[1]]) * scale
    shift_grads = jnp.stack([first[2], second[2]]) * scale
    return (outcome, state_grad, mixer_grads, stencil_grads, shift_grads)


def solution(mesh):
    placed = (
        P("batch", "tile", None, None, None),
        P("batch", "tile", None, None, None),
        P(),
        P(),
        P(),
        P(),
        P(),
    )
    return jax.shard_map(
        shards,
        mesh=mesh,
        in_specs=placed,
        out_specs=(
            P("batch", "tile", None, None, None),
            P("batch", "tile", None, None, None),
            P(),
            P(),
            P(),
        ),
        check_vma=False,
    )
```

profile of v0, /device:TPU:0, one launch (start us, length us, event | category | flops | bytes accessed | tf_op | source)
XLA Modules:
  0.0 484.4 jit_solution(14391664478822716902)
XLA Ops:
  14.5 7.3 %all-to-all-start = ((bf16[1,8,2,16,256]{4,3,2,0,1:T(8,128)(2,1)}), bf16[1,8,2,16,256]{4,3,2,0,1:T(8,128)(2,1)S(1)}, u32[]{:S(2)}, u32[]{:S(2)}) async-start(bf16[1,8,2,16,256]{4,3,2,0,1:T(8,128)(2,1)} %bitcast.10), calls=%async_computation | async-start | bytes 262144 | tf_op jit(solution)/shard_map/all_to_all | solution.py:209
  31.3 8.4 %constant_dynamic-update-slice_fusion.1 = (bf16[1,8,16,18,256]{4,0,3,2,1:T(2,128)(2,1)S(1)}, f32[1,8,16,16,256]{4,0,3,2,1:T(1,128)}, bf16[1,8,16,16,256]{4,0,3,2,1:T(2,128)(2,1)S(1)}) fusion(bf16[1,8,16,18,256]{4,0,3,2,1:T(2,128)(2,1)S(1)} %get-tuple-element.225, bf16[1,8,16,16,256]{4,3,2,1,0:T(8,128)(2,1)S(1)} %copy-done.18), kind=kLoop, calls=%fused_computation.218 | loop fusion | flops 524288 | bytes 7340032
  40.5 19.6 %add_convert_fusion.1 = bf16[1,8,16,16,256]{4,0,3,2,1:T(2,128)(2,1)S(1)} fusion(f32[256]{0:T(256)S(1)} %bitcast.332, f32[256]{0:T(256)S(1)} %bitcast.334, f32[256]{0:T(256)S(1)} %bitcast.336, f32[256]{0:T(256)S(1)} %bitcast.338, f32[256]{0:T(256)S(1)} %bitcast.340, f32[256]{0:T(256)S(1)} %bitcast.330, f32[256]{0:T(256)S(1)} %bitcast.342, ...), kind=kLoop, calls=%fused_computation.85 | loop fusion | flops 18350080 | bytes 3564544 | tf_op jit(solution)/shard_map/convert_element_type | solution.py:123
  67.2 4.3 all-to-all-start.1
  71.5 17.2 %broadcast_multiply_fusion.17 = (f32[1,8,16,16,256]{4,0,3,2,1:T(1,128)}, f32[1,8,16,16,256]{4,0,3,2,1:T(1,128)}, f32[1,8,16,16,256]{4,0,3,2,1:T(1,128)}, f32[1,8...) fusion(f32[256]{0:T(256)} %bitcast.348, ...), kind=kLoop, calls=%fused_computation.111 | loop fusion | flops 3670016 | bytes 16784384 | tf_op jit(solution)/shard_map/mul | solution.py:61
  90.2 3.1 copy.350
  100.6 3.4 constant_dynamic-update-slice_fusion.4
  104.8 19.6 %add_convert_fusion = bf16[1,8,16,16,256]{4,0,3,2,1:T(2,128)(2,1)S(1)} fusion(bf16[1,8,16,16,256]{4,0,3,2,1:T(2,128)(2,1)S(1)} %get-tuple-element.199, f32[256]{0:T(256)S(1)} %bitcast.364, f32[256]{0:T(256)S(1)} %bitcast.361, f32[256]{0:T(256)S(1)} %bitcast.351, f32[256]{0:T(256)S(1)} %bitcast.353, f32[256]{0:T(256)S(1)} %bitcast.355, f32[256]{0:T(256)S(1)} %bitcast.362, ...), kind=kLoop, calls=%fused_computation.82 | loop fusion | flops 18350080 | bytes 3564544 | tf_op jit(solution)/shard_map/convert_element_type | solution.py:128
  124.5 23.5 %multiply_reduce_fusion = (f32[256]{0:T(256)S(1)}, f32[256]{0:T(256)S(1)}, f32[256]{0:T(256)S(1)}, f32[256]{0:T(256)S(1)}, f32[256]{0:T(256)S(1)}, /*index=5*/f3...) fusion(bf16[1,8,1,18,256]{4,0,3,2,1:T(2,128)(2,1)S(1)} %copy.30, ...), kind=kLoop, calls=%fused_computation.64 | loop fusion | flops 17823744 | bytes 8808448 | tf_op jit(solution)/shard_map/reduce_sum | solution.py:76
  148.1 14.4 %pad_add_fusion.1 = f32[1,8,18,18,256]{4,0,3,2,1:T(1,128)S(1)} fusion(f32[1,8,16,16,256]{4,0,3,2,1:T(1,128)S(1)} %get-tuple-element.179, f32[1,8,16,16,256]{4,0,3,2,1:T(1,128)S(1)} %copy-done.15, f32[1,8,16,16,256]{4,0,3,2,1:T(1,128)S(1)} %copy-done.14, f32[1,8,16,16,256]{4,0,3,2,1:T(1,128)S(1)} %copy-done.13, f32[1,8,16,16,256]{4,0,3,2,1:T(1,128)S(1)} %copy-done.12, ...), kind=kLoop, calls=%fused_computation.17 | loop fusion | flops 5308416 | bytes 21528576 | tf_op jit(solution)/shard_map/add | solution.py:60
  162.5 3.7 slice.782
  177.2 6.3 %all-to-all-start.2 = ((f32[1,8,2,16,256]{4,3,2,0,1:T(8,128)}), f32[1,8,2,16,256]{4,3,2,0,1:T(8,128)}, u32[]{:S(2)}, u32[]{:S(2)}) async-start(f32[1,8,2,16,256]{4,3,2,0,1:T(8,128)} %bitcast.320), calls=%async_computation.2 | async-start | bytes 524288 | tf_op jit(solution)/shard_map/all_to_all | solution.py:231
  183.5 3.0 fusion.1
  186.6 6.1 %scatter_fusion = f32[32,16,256]{2,1,0:T(8,128)S(1)} fusion(f32[32,16,256]{2,1,0:T(8,128)S(1)} %broadcast.680.clone, s32[64]{0:T(128)S(1)} %copy-done.80, f32[64,16,256]{2,1,0:T(8,128)} %select_bitcast_fusion.1), kind=kCustom, calls=%fused_computation.8 | custom fusion | flops 262144 | bytes 3145984 | tf_op jit(solution)/shard_map/scatter-add | solution.py:242
  192.8 2.7 convolution_bitcast_fusion
  210.2 17.4 %broadcast_multiply_fusion.16 = (f32[1,8,16,16,256]{4,0,3,2,1:T(1,128)S(1)}, f32[1,8,16,16,256]{4,0,3,2,1:T(1,128)S(1)}, f32[1,8,16,16,256]{4,0,3,2,1:T(1,128)S(...) fusion(f32[256]{0:T(256)S(1)} %bitcast.347, ...), kind=kLoop, calls=%fused_computation.110 | loop fusion | flops 4194304 | bytes 18882560 | tf_op jit(solution)/shard_map/mul | solution.py:61
  227.7 25.6 %multiply_reduce_fusion.9 = (f32[256]{0:T(256)S(1)}, f32[256]{0:T(256)S(1)}, f32[256]{0:T(256)S(1)}, f32[256]{0:T(256)S(1)}, f32[256]{0:T(256)S(1)}, /*index=5*/...) fusion(bf16[1,8,1,18,256]{4,0,3,2,1:T(2,128)(2,1)S(1)} %copy-done.24, ...), kind=kLoop, calls=%fused_computation.73 | loop fusion | flops 18872064 | bytes 7759872 | tf_op jit(solution)/shard_map/reduce_sum | solution.py:76
  253.3 15.1 %pad_add_fusion = f32[1,8,18,18,256]{4,0,3,2,1:T(1,128)S(1)} fusion(f32[1,8,16,16,256]{4,0,3,2,1:T(1,128)S(1)} %get-tuple-element.186, f32[1,8,16,16,256]{4,0,3,2,1:T(1,128)S(1)} %get-tuple-element.185, f32[1,8,16,16,256]{4,0,3,2,1:T(1,128)S(1)} %get-tuple-element.184, f32[1,8,16,16,256]{4,0,3,2,1:T(1,128)S(1)} %get-tuple-element.183, ...), kind=kLoop, calls=%fused_computation.16 | loop fusion | flops 5308416 | bytes 21528576 | tf_op jit(solution)/shard_map/add | solution.py:60
  276.4 6.0 %all-to-all-start.3 = ((f32[1,8,2,16,256]{4,3,2,0,1:T(8,128)}), f32[1,8,2,16,256]{4,3,2,0,1:T(8,128)S(1)}, u32[]{:S(2)}, u32[]{:S(2)}) async-start(f32[1,8,2,16,256]{4,3,2,0,1:T(8,128)} %bitcast.101), calls=%async_computation.3 | async-start | bytes 524288 | tf_op jit(solution)/shard_map/all_to_all | solution.py:231
  282.5 2.7 convolution_bitcast_fusion.1
  285.2 3.7 slice.799
  291.3 6.1 %scatter_fusion.2 = f32[32,16,256]{2,1,0:T(8,128)S(1)} fusion(f32[32,16,256]{2,1,0:T(8,128)S(1)} %broadcast.680, s32[64]{0:T(128)S(1)} %copy-done.80, f32[64,16,256]{2,1,0:T(8,128)} %select_bitcast_fusion), kind=kCustom, calls=%fused_computation.10 | custom fusion | flops 262144 | bytes 3145984 | tf_op jit(solution)/shard_map/scatter-add | solution.py:242
  297.5 121.3 %all-reduce.22.cloned.1.call-done = (f32[1,256,256]{2,1,0:T(8,128)}, f32[1,256,256]{2,1,0:T(8,128)}) async-done(((f32[1,256,256]{2,1,0:T(8,128)}, f32[1,256,256]{2,1,0:T(8,128)}), (f32[1,256,256]{2,1,0:T(8,128)}, f32[1,256,256]{2,1,0:T(8,128)})) %all-reduce.22.cloned.1.call-update) | async-done | bytes 524304 | tf_op jit(solution)/shard_map/psum | solution.py:255
  436.3 39.6 %all-reduce.18 = (f32[1,9,256]{2,1,0:T(8,128)S(1)}, f32[1,9,256]{2,1,0:T(8,128)S(1)}, f32[1,256]{1,0:T(1,128)S(1)}, f32[1,256]{1,0:T(1,128)S(1)}) all-reduce(f32[1,9,256]{2,1,0:T(8,128)S(1)} %bitcast.328, f32[1,9,256]{2,1,0:T(8,128)S(1)} %bitcast.329, ...), channel_id=1, replica_groups=mesh['tile'=8,'batch'=4] {'tile','batch'}, use_global_device_ids=true, to_apply=%region_30.35 | all-reduce | flops 5120 | bytes 40960 | tf_op jit(solution)/shard_map/psum | solution.py:255
  (306 shorter events, 87.9 us)
Async XLA Ops:
  8.6 17.6 %copy-start.31 = (f32[2,9,256]{2,0,1:T(2,128)S(1)}, f32[2,9,256]{2,0,1:T(2,128)}, u32[]{:S(2)}) copy-start(f32[2,9,256]{2,0,1:T(2,128)} %param.36) | copy-start | bytes 55300
  11.6 18.2 %copy-start.32 = (pred[64]{0:T(512)(128)(4,1)}, pred[64]{0:T(512)(128)(4,1)S(1)}, u32[]{:S(2)}) copy-start(pred[64]{0:T(512)(128)(4,1)S(1)} %get-tuple-element.161) | copy-start | bytes 196
  11.6 18.2 %copy-start.69 = (pred[64]{0:T(512)(128)(4,1)}, pred[64]{0:T(512)(128)(4,1)S(1)}, u32[]{:S(2)}) copy-start(pred[64]{0:T(512)(128)(4,1)S(1)} %get-tuple-element.159) | copy-start | bytes 196
  14.5 14.6 %all-to-all-start = ((bf16[1,8,2,16,256]{4,3,2,0,1:T(8,128)(2,1)}), bf16[1,8,2,16,256]{4,3,2,0,1:T(8,128)(2,1)S(1)}, u32[]{:S(2)}, u32[]{:S(2)}) async-start(bf16[1,8,2,16,256]{4,3,2,0,1:T(8,128)(2,1)} %bitcast.10), calls=%async_computation | async-start | bytes 262144 | tf_op jit(solution)/shard_map/all_to_all | solution.py:209
  39.9 20.2 %copy-start.21 = (bf16[1,8,1,18,256]{4,0,3,2,1:T(2,128)(2,1)}, bf16[1,8,1,18,256]{4,0,3,2,1:T(2,128)(2,1)S(1)}, u32[]{:S(2)}) copy-start(bf16[1,8,1,18,256]{4,0,3,2,1:T(2,128)(2,1)S(1)} %copy.279) | copy-start | bytes 221188
  40.1 20.1 %copy-start.23 = (bf16[1,8,1,18,256]{4,0,3,2,1:T(2,128)(2,1)}, bf16[1,8,1,18,256]{4,0,3,2,1:T(2,128)(2,1)S(1)}, u32[]{:S(2)}) copy-start(bf16[1,8,1,18,256]{4,0,3,2,1:T(2,128)(2,1)S(1)} %copy.284) | copy-start | bytes 221188
  40.4 19.8 %copy-start.4 = (bf16[1,8,16,18,256]{4,0,3,2,1:T(2,128)(2,1)}, bf16[1,8,16,18,256]{4,0,3,2,1:T(2,128)(2,1)S(1)}, u32[]{:S(2)}) copy-start(bf16[1,8,16,18,256]{4,0,3,2,1:T(2,128)(2,1)S(1)} %get-tuple-element.223) | copy-start | bytes 3538948
  40.4 19.8 %copy-start.27 = (bf16[1,8,16,1,256]{4,0,3,2,1:T(2,128)(2,1)}, bf16[1,8,16,1,256]{4,0,3,2,1:T(2,128)(2,1)S(1)}, u32[]{:S(2)}) copy-start(bf16[1,8,16,1,256]{4,0,3,2,1:T(2,128)(2,1)S(1)} %get-tuple-element.224) | copy-start | bytes 196612
  67.2 26.2 %all-to-all-start.1 = ((bf16[1,8,2,16,256]{4,3,2,0,1:T(8,128)(2,1)}), bf16[1,8,2,16,256]{4,3,2,0,1:T(8,128)(2,1)S(1)}, u32[]{:S(2)}, u32[]{:S(2)}) async-start(bf16[1,8,2,16,256]{4,3,2,0,1:T(8,128)(2,1)} %bitcast.321), calls=%async_computation.1 | async-start | bytes 262144 | tf_op jit(solution)/shard_map/all_to_all | solution.py:209
  104.8 19.7 %copy-start.2 = (f32[2048,256]{1,0:T(8,128)S(1)}, f32[2048,256]{1,0:T(8,128)}, u32[]{:S(2)}) copy-start(f32[2048,256]{1,0:T(8,128)} %get-tuple-element.260) | copy-start | bytes 6291460
  104.8 43.2 %copy-start.16 = (f32[1,8,16,16,256]{4,0,3,2,1:T(1,128)S(1)}, f32[1,8,16,16,256]{4,0,3,2,1:T(1,128)}, u32[]{:S(2)}) copy-start(f32[1,8,16,16,256]{4,0,3,2,1:T(1,128)} %get-tuple-element.194) | copy-start | bytes 6291460
  104.8 43.2 %copy-start.17 = (f32[1,8,16,16,256]{4,0,3,2,1:T(1,128)S(1)}, f32[1,8,16,16,256]{4,0,3,2,1:T(1,128)}, u32[]{:S(2)}) copy-start(f32[1,8,16,16,256]{4,0,3,2,1:T(1,128)} %get-tuple-element.195) | copy-start | bytes 6291460
  124.5 23.5 %copy-start.11 = (f32[1,8,16,16,256]{4,0,3,2,1:T(1,128)S(1)}, f32[1,8,16,16,256]{4,0,3,2,1:T(1,128)}, u32[]{:S(2)}) copy-start(f32[1,8,16,16,256]{4,0,3,2,1:T(1,128)} %get-tuple-element.189) | copy-start | bytes 6291460
  124.5 23.5 %copy-start.12 = (f32[1,8,16,16,256]{4,0,3,2,1:T(1,128)S(1)}, f32[1,8,16,16,256]{4,0,3,2,1:T(1,128)}, u32[]{:S(2)}) copy-start(f32[1,8,16,16,256]{4,0,3,2,1:T(1,128)} %get-tuple-element.190) | copy-start | bytes 6291460
  124.5 23.5 %copy-start.13 = (f32[1,8,16,16,256]{4,0,3,2,1:T(1,128)S(1)}, f32[1,8,16,16,256]{4,0,3,2,1:T(1,128)}, u32[]{:S(2)}) copy-start(f32[1,8,16,16,256]{4,0,3,2,1:T(1,128)} %get-tuple-element.191) | copy-start | bytes 6291460
  124.5 23.5 %copy-start.14 = (f32[1,8,16,16,256]{4,0,3,2,1:T(1,128)S(1)}, f32[1,8,16,16,256]{4,0,3,2,1:T(1,128)}, u32[]{:S(2)}) copy-start(f32[1,8,16,16,256]{4,0,3,2,1:T(1,128)} %get-tuple-element.192) | copy-start | bytes 6291460
  124.5 23.5 %copy-start.15 = (f32[1,8,16,16,256]{4,0,3,2,1:T(1,128)S(1)}, f32[1,8,16,16,256]{4,0,3,2,1:T(1,128)}, u32[]{:S(2)}) copy-start(f32[1,8,16,16,256]{4,0,3,2,1:T(1,128)} %get-tuple-element.193) | copy-start | bytes 6291460
  177.2 18.3 %all-to-all-start.2 = ((f32[1,8,2,16,256]{4,3,2,0,1:T(8,128)}), f32[1,8,2,16,256]{4,3,2,0,1:T(8,128)}, u32[]{:S(2)}, u32[]{:S(2)}) async-start(f32[1,8,2,16,256]{4,3,2,0,1:T(8,128)} %bitcast.320), calls=%async_computation.2 | async-start | bytes 524288 | tf_op jit(solution)/shard_map/all_to_all | solution.py:231
  210.1 17.5 %copy-start.5 = (bf16[1,8,16,18,256]{4,0,3,2,1:T(2,128)(2,1)S(1)}, bf16[1,8,16,18,256]{4,0,3,2,1:T(2,128)(2,1)}, u32[]{:S(2)}) copy-start(bf16[1,8,16,18,256]{4,0,3,2,1:T(2,128)(2,1)} %copy-done.4) | copy-start | bytes 3538948
  210.1 17.5 %copy-start.19 = (bf16[1,8,16,16,256]{4,3,2,1,0:T(8,128)(2,1)S(1)}, bf16[1,8,16,16,256]{4,3,2,1,0:T(8,128)(2,1)}, u32[]{:S(2)}) copy-start(bf16[1,8,16,16,256]{4,3,2,1,0:T(8,128)(2,1)} %param.31) | copy-start | bytes 3145732
  210.1 17.5 %copy-start.22 = (bf16[1,8,1,18,256]{4,0,3,2,1:T(2,128)(2,1)S(1)}, bf16[1,8,1,18,256]{4,0,3,2,1:T(2,128)(2,1)}, u32[]{:S(2)}) copy-start(bf16[1,8,1,18,256]{4,0,3,2,1:T(2,128)(2,1)} %copy-done.21) | copy-start | bytes 221188
  210.1 17.5 %copy-start.24 = (bf16[1,8,1,18,256]{4,0,3,2,1:T(2,128)(2,1)S(1)}, bf16[1,8,1,18,256]{4,0,3,2,1:T(2,128)(2,1)}, u32[]{:S(2)}) copy-start(bf16[1,8,1,18,256]{4,0,3,2,1:T(2,128)(2,1)} %copy-done.23) | copy-start | bytes 221188
  276.4 144.3 %all-to-all-start.3 = ((f32[1,8,2,16,256]{4,3,2,0,1:T(8,128)}), f32[1,8,2,16,256]{4,3,2,0,1:T(8,128)S(1)}, u32[]{:S(2)}, u32[]{:S(2)}) async-start(f32[1,8,2,16,256]{4,3,2,0,1:T(8,128)} %bitcast.101), calls=%async_computation.3 | async-start | bytes 524288 | tf_op jit(solution)/shard_map/all_to_all | solution.py:231
  282.4 136.5 %all-reduce.22.cloned.1.call-start = ((), (), s32[]{:S(2)}) async-start(), calls=%async_computation.4 | async-start | bytes 1048576 | tf_op jit(solution)/shard_map/psum | solution.py:255
  (62 other events, 429.0 us)
Sparse Core Ops, SparseCore 0:
  289.3 129.5 all-reduce.21
where the time goes:
time: 494 us; the launch traced here: 484 us
  other arithmetic  220 us (45%)
  waiting for transfers between devices  124 us (25%)
  local copies, waits for them, and re-layouts  48.7 us (10%)
  blocking collectives  39.6 us (8%)
  starting transfers between devices  23.9 us (5%)
  between operations  16.3 us (3%)
  matrix products  11.9 us (2%)
    psum x1, waiting for transfers between devices, shards(): lax.psum((first[0], first[1], first[2], second[0], second[1], second[2]),...  121 us
    reduce_sum x2, other arithmetic, stencil_grad(): terms.append(jnp.sum(widened * window, axis=(0, 1, 2, 3)))  49.1 us
    psum x1, blocking collectives, shards(): lax.psum((first[0], first[1], first[2], second[0], second[1], second[2]),...  39.6 us
    mul x2, other arithmetic, stencil_back(): kernel[3 * row_at + col_at] * widened  34.6 us
    add x2, other arithmetic, stencil_back(): running + jnp.pad(kernel[3 * row_at + col_at] * widened, ((0, 0), (0, 0),...  29.5 us
    convert_element_type x1, other arithmetic, block_pass(): conv_first = stencil_apply(padded_in, stencils[0]).astype(jnp.bfloat16)  19.6 us
    convert_element_type x1, other arithmetic, block_pass(): conv_second = stencil_apply(padded_mid, stencils[1]).astype(jnp.bfloat16)  19.6 us
    unnamed x182, local copies, waits for them, and re-layouts  17.8 us
  transfers between devices with their start and end apart: 5, of which 2 were waited for; matrix products, arithmetic and copies ran while one was open for 11% of the time, Pallas kernels for 0%

commit v1 on v0

v1 whole, which is shorter than its diff:
```python
import functools
import math

import jax
import jax.numpy as jnp
from jax import lax
from jax.experimental import pallas as pl
from jax.experimental.pallas import tpu as pltpu
from jax.sharding import PartitionSpec as P

CAP = 2
MESH = pl.DeviceIdType.MESH
SQRT_HALF = 0.7071067811865476
INV_ROOT_TAU = 0.3989422804014327
F32 = jnp.float32
BF16 = jnp.bfloat16


def iota(shape, dim):
    return lax.broadcasted_iota(jnp.int32, shape, dim)


def dot(a, b, ca=1, cb=0):
    return lax.dot_general(a, b, (((ca,), (cb,)), ((), ())), preferred_element_type=F32)


def one_hot(mask):
    return jnp.where(mask, 1.0, 0.0).astype(BF16)


def kernel(
    groups,
    scale,
    states,
    cotangent,
    slots,
    codes,
    mixers,
    stencils,
    shifts,
    outcome,
    state_grad,
    sums,
    pad_in,
    pad_mid,
    wide_second,
    wide_first,
    back_second,
    back_first,
    slope,
    conv,
    cot,
    rims,
    parts,
    fetch_map,
    send_map,
    outbox,
    inbox,
    send_sem,
    recv_sem,
):
    tiles, side, channels = states.shape[1], states.shape[2], states.shape[4]
    line = side * tiles
    edge = 4 * line
    mail = CAP * side
    cells = side * line
    me = lax.axis_index("tile")

    def peer_of(k):
        return lax.rem(me + k, groups)

    barrier = pltpu.get_barrier_semaphore()

    def greet(k, _):
        pl.semaphore_signal(
            barrier, inc=1, device_id={"tile": peer_of(k)}, device_id_type=MESH
        )
        return 0

    lax.fori_loop(1, groups, greet, 0)

    def copy_to(x, peer):
        return pltpu.make_async_remote_copy(
            src_ref=outbox.at[x, peer],
            dst_ref=inbox.at[x, me],
            send_sem=send_sem.at[x, peer],
            recv_sem=recv_sem.at[x, me],
            device_id={"tile": peer},
            device_id_type=MESH,
        )

    def copy_from(x, peer):
        return pltpu.make_async_remote_copy(
            src_ref=outbox.at[x, peer],
            dst_ref=inbox.at[x, peer],
            send_sem=send_sem.at[x, peer],
            recv_sem=recv_sem.at[x, peer],
            device_id={"tile": peer},
            device_id_type=MESH,
        )

    def send(x):
        def body(k, _):
            copy_to(x, peer_of(k)).start()
            return 0

        lax.fori_loop(1, groups, body, 0)

    def receive(x):
        def body(k, _):
            copy_from(x, peer_of(k)).wait_recv()
            return 0

        lax.fori_loop(1, groups, body, 0)

    def finish_sends(x):
        def body(k, _):
            copy_to(x, peer_of(k)).wait_send()
            return 0

        lax.fori_loop(1, groups, body, 0)

    entries = 8 * tiles

    def block_columns(p):
        rows = pl.ds(p * tiles, tiles)
        slot = slots[rows, :]
        code = codes[rows, :]
        column = lambda v: jnp.concatenate([v[:, d : d + 1] for d in range(8)], axis=0)
        slot, code = column(slot), column(code)
        owner = lax.div(slot, tiles)
        local = slot - owner * tiles
        base = lax.shift_right_logical(code, 1) * line + local
        flip = code & 1
        above = iota((entries, entries), 0)
        aside = iota((entries, entries), 1)
        owner_row = jnp.sum(
            jnp.where(above == aside, jnp.broadcast_to(owner, (entries, entries)), 0),
            axis=0,
            keepdims=True,
        )
        place = jnp.sum(
            jnp.where((owner == owner_row) & (aside < above), 1, 0), axis=1, keepdims=True
        )
        return owner, base, flip, place

    def send_rows(p, _):
        owner, base, _, place = block_columns(p)
        for k in range(CAP):
            hit = (owner == me) & (place == k) & (p != me)
            found = jnp.sum(jnp.where(hit, base + 1, 0), axis=0, keepdims=True) - 1
            found = jnp.where(found < 0, -edge, found)
            want = found + tiles * iota((side, 1), 0)
            send_map[pl.ds(pl.multiple_of(p * mail + k * side, side), side), :] = one_hot(
                iota((side, edge), 1) == want
            )
        return 0

    lax.fori_loop(0, groups, send_rows, 0)

    owner, base, flip, place = block_columns(me)
    remote = owner != me
    base = jnp.where(remote, edge + (owner * CAP + place) * side, base)
    stride = jnp.where(remote, 1, tiles)
    pool = edge + groups * mail
    for d in range(8):
        rows = slice(d * tiles, (d + 1) * tiles)
        base_d, stride_d, flip_d = base[rows], stride[rows], flip[rows]
        if d < 4:
            at = iota((side, tiles, pool), 0)
            at = jnp.where(flip_d[None] == 1, side - 1 - at, at)
            hot = iota((side, tiles, pool), 2) == base_d[None] + at * stride_d[None]
            fetch_map[d * line : (d + 1) * line, :] = (
                jnp.where(hot, 1.0, 0.0).reshape(line, pool).astype(BF16)
            )
    corner = []
    for d in range(4, 8):
        rows = slice(d * tiles, (d + 1) * tiles)
        want = base[rows] + jnp.where(flip[rows] == 1, (side - 1) * stride[rows], 0)
        corner.append(jnp.where(iota((tiles, pool), 1) == want, 1.0, 0.0))
    fetch_map[edge : edge + 4 * tiles, :] = jnp.concatenate(corner, axis=0).astype(BF16)

    turn = one_hot(
        iota((line, line), 1)
        == lax.rem(iota((line, line), 0), tiles) * side + lax.div(iota((line, line), 0), tiles)
    )
    turn_back = one_hot(
        iota((line, line), 1)
        == lax.rem(iota((line, line), 0), side) * tiles + lax.div(iota((line, line), 0), side)
    )

    for x in range(4):
        inbox[x, me] = jnp.zeros((mail, channels), BF16)
    for wide in (wide_second, wide_first):
        for rows in (slice(0, 2), slice(side + 2, side + 4)):
            wide[rows] = jnp.zeros((2, side + 4, tiles, channels), F32)
            wide[2 : side + 2, rows] = jnp.zeros((side, 2, tiles, channels), F32)

    def take_states(y, _):
        x = states[0, :, y].reshape(line, channels)
        pad_in[y + 1, 1 : side + 1] = dot(turn, x).reshape(side, tiles, channels)
        return 0

    lax.fori_loop(0, side, take_states, 0)

    def take_rims(pad):
        inner = slice(1, side + 1)
        for e, piece in enumerate(
            (pad[1, inner], pad[inner, side], pad[side, inner], pad[inner, 1])
        ):
            rims[e * line : (e + 1) * line, :] = piece.reshape(line, channels).astype(BF16)

    def post_rims(x, pad):
        take_rims(pad)
        out = dot(send_map[...], rims[...])
        outbox[x] = out.astype(BF16).reshape(groups, mail, channels)
        send(x)

    def fill_halo(x, pad):
        panels = dot(fetch_map[:, :edge], rims[...]) + dot(
            fetch_map[:, edge:], inbox[x].reshape(groups * mail, channels)
        )
        inner = slice(1, side + 1)
        strip = lambda d: panels[d * line : (d + 1) * line].reshape(side, tiles, channels)
        pad[0, inner] = strip(0)
        pad[inner, side + 1] = strip(1)
        pad[side + 1, inner] = strip(2)
        pad[inner, 0] = strip(3)
        spot = lambda d: panels[edge + d * tiles : edge + (d + 1) * tiles]
        pad[0, side + 1] = spot(0)
        pad[side + 1, side + 1] = spot(1)
        pad[side + 1, 0] = spot(2)
        pad[0, 0] = spot(3)

    halves = [slice(h, min(h + 128, channels)) for h in range(0, channels, 128)]

    def convolve(pad, layer):
        def body(y, _):
            pieces = []
            for half in halves:
                total = None
                for a in range(3):
                    for b in range(3):
                        tap = stencils[layer, 3 * a + b : 3 * a + b + 1, half]
                        term = tap[None] * pad[y + a, b : b + side, :, half]
                        total = term if total is None else total + term
                pieces.append(total.reshape(line, total.shape[2]).astype(BF16))
            conv[pl.ds(pl.multiple_of(y * line, line), line), :] = jnp.concatenate(pieces, axis=1)
            return 0

        lax.fori_loop(0, side, body, 0)

    def convolve_back(wide, out, layer):
        def body(y, _):
            for half in halves:
                total = None
                for a in range(3):
                    for b in range(3):
                        tap = stencils[layer, 3 * a + b : 3 * a + b + 1, half]
                        term = tap[None] * wide[y + 2 - a, 2 - b : 2 - b + side + 2, :, half]
                        total = term if total is None else total + term
                out[y, :, :, half] = total
            return 0

        lax.fori_loop(0, side + 2, body, 0)

    extra = 2 * channels

    def stencil_sums(wide, pad, layer):
        for half in halves:

            def body(y, held):
                grad = wide[y + 2, 2 : side + 2, :, half]
                new = []
                for a in range(3):
                    for b in range(3):
                        term = jnp.sum(grad * pad[y + a, b : b + side, :, half], axis=0)
                        new.append(held[3 * a + b] + term)
                return tuple(new)

            held = lax.fori_loop(
                0, side, body, tuple(jnp.zeros((tiles, 128), F32) for _ in range(9))
            )
            for tap in range(9):
                row = extra + 9 * layer + tap
                sums[row : row + 1, half] = jnp.sum(held[tap], axis=0, keepdims=True) * scale

    def post_parts(x, back):
        inner = slice(1, side + 1)
        for d, piece in enumerate(
            (back[0, inner], back[inner, side + 1], back[side + 1, inner], back[inner, 0])
        ):
            parts[d * line : (d + 1) * line, :] = piece.reshape(line, channels).astype(BF16)
        parts[edge : edge + 4 * tiles, :] = jnp.concatenate(
            [back[0, side + 1], back[side + 1, side + 1], back[side + 1, 0], back[0, 0]], axis=0
        ).astype(BF16)
        out = dot(fetch_map[:, edge:], parts[...], 0, 0)
        outbox[x] = out.astype(BF16).reshape(groups, mail, channels)
        send(x)

    def add_rims(back, grads):
        inner = slice(1, side + 1)
        strip = lambda e: grads[e * line : (e + 1) * line].reshape(side, tiles, channels)
        back[1, inner] = back[1, inner] + strip(0)
        back[inner, side] = back[inner, side] + strip(1)
        back[side, inner] = back[side, inner] + strip(2)
        back[inner, 1] = back[inner, 1] + strip(3)

    def add_local(back):
        add_rims(back, dot(fetch_map[:, :edge], parts[...], 0, 0))

    def add_remote(x, back):
        add_rims(back, dot(send_map[...], inbox[x].reshape(groups * mail, channels), 0, 0))

    step = max(s for s in (1, 2, 4) if side % s == 0)
    chunk = step * line

    pl.semaphore_wait(barrier, groups - 1)
    post_rims(0, pad_in)

    def take_cotangent(c, total):
        for r in range(step):
            y = c * step + r
            x = dot(turn, cotangent[0, :, y].reshape(line, channels))
            total = total + jnp.sum(x.reshape(side, tiles, channels), axis=0)
            cot[pl.ds(pl.multiple_of(y * line, line), line), :] = x.astype(BF16)
        mine = cot[pl.ds(pl.multiple_of(c * chunk, chunk), chunk), :]
        grad = dot(mine, mixers[1], 1, 1).astype(BF16).astype(F32)
        wide_second[pl.ds(c * step + 2, step), 2 : side + 2] = grad.reshape(
            step, side, tiles, channels
        )
        return total

    total = lax.fori_loop(0, side // step, take_cotangent, jnp.zeros((tiles, channels), F32))
    row = extra + 19
    sums[row : row + 1, :] = jnp.sum(total, axis=0, keepdims=True) * scale
    sums[row + 1 :, :] = jnp.zeros((sums.shape[0] - row - 1, channels), F32)

    convolve_back(wide_second, back_second, 1)
    post_parts(1, back_second)
    add_local(back_second)

    receive(0)
    fill_halo(0, pad_in)
    convolve(pad_in, 0)

    def mix_first(c, _):
        rows = pl.ds(pl.multiple_of(c * chunk, chunk), chunk)
        hidden = dot(conv[rows, :], mixers[0]) + shifts[0:1, :]
        half_cdf = 0.5 * (1.0 + lax.erf(hidden * SQRT_HALF))
        active = (hidden * half_cdf).astype(BF16).astype(F32)
        slope[rows, :] = half_cdf + hidden * jnp.exp(-0.5 * hidden * hidden) * INV_ROOT_TAU
        pad_mid[pl.ds(c * step + 1, step), 1 : side + 1] = active.reshape(
            step, side, tiles, channels
        )
        return 0

    lax.fori_loop(0, side // step, mix_first, 0)
    post_rims(2, pad_mid)

    receive(1)
    add_remote(1, back_second)

    def grad_first(c, total):
        rows = pl.ds(pl.multiple_of(c * chunk, chunk), chunk)
        active_grad = back_second[pl.ds(c * step + 1, step), 1 : side + 1].reshape(chunk, channels)
        hidden_grad = (active_grad * slope[rows, :]).astype(BF16)
        wide_sum = hidden_grad.astype(F32).reshape(step * side, tiles, channels)
        total = total + jnp.sum(wide_sum, axis=0)
        grad = dot(hidden_grad, mixers[0], 1, 1).astype(BF16).astype(F32)
        wide_first[pl.ds(c * step + 2, step), 2 : side + 2] = grad.reshape(
            step, side, tiles, channels
        )
        term = dot(conv[rows, :], hidden_grad, 0, 0) * scale
        sums[0:channels, :] = jnp.where(c == 0, 0.0, sums[0:channels, :]) + term
        return total

    sums[0 : 2 * channels, :] = jnp.zeros((2 * channels, channels), F32)
    total = lax.fori_loop(0, side // step, grad_first, jnp.zeros((tiles, channels), F32))
    row = extra + 18
    sums[row : row + 1, :] = jnp.sum(total, axis=0, keepdims=True) * scale

    convolve_back(wide_first, back_first, 0)
    post_parts(3, back_first)
    add_local(back_first)
    stencil_sums(wide_first, pad_in, 0)

    receive(2)
    fill_halo(2, pad_mid)
    convolve(pad_mid, 1)
    stencil_sums(wide_second, pad_mid, 1)

    def mix_second(c, _):
        rows = pl.ds(pl.multiple_of(c * chunk, chunk), chunk)
        sums[channels : 2 * channels, :] = (
            sums[channels : 2 * channels, :] + dot(conv[rows, :], cot[rows, :], 0, 0) * scale
        )
        held = pad_in[pl.ds(c * step + 1, step), 1 : side + 1].reshape(chunk, channels)
        result = (held + dot(conv[rows, :], mixers[1]) + shifts[1:2, :]).astype(BF16)
        for r in range(step):
            turned = dot(turn_back, result[r * line : (r + 1) * line])
            outcome[0, :, c * step + r] = turned.astype(BF16).reshape(tiles, side, channels)
        return 0

    lax.fori_loop(0, side // step, mix_second, 0)

    receive(3)
    add_remote(3, back_first)

    def put_grad(y, _):
        inner = back_first[y + 1, 1 : side + 1].reshape(line, channels)
        rows = pl.ds(pl.multiple_of(y * line, line), line)
        result = (cot[rows, :].astype(F32) + inner).astype(BF16)
        turned = dot(turn_back, result)
        state_grad[0, :, y] = turned.astype(BF16).reshape(tiles, side, channels)
        return 0

    lax.fori_loop(0, side, put_grad, 0)
    for x in range(4):
        finish_sends(x)


def shards(states, cotangent, beside_slot, beside_code, mixers, stencils, shifts):
    samples, tiles, side, _, channels = states.shape
    groups = lax.axis_size("tile")
    total = samples * tiles * side * side * groups * lax.axis_size("batch")
    scale = 1.0 / math.sqrt(total)
    rows = -(-(2 * channels + 20) // 8) * 8
    line = side * tiles
    edge = 4 * line
    mail = CAP * side
    vmem = pl.BlockSpec(memory_space=pltpu.VMEM)
    outcome, state_grad, sums = pl.pallas_call(
        functools.partial(kernel, groups, scale),
        out_shape=(
            jax.ShapeDtypeStruct(states.shape, BF16),
            jax.ShapeDtypeStruct(states.shape, BF16),
            jax.ShapeDtypeStruct((rows, channels), F32),
        ),
        in_specs=[vmem] * 7,
        out_specs=(vmem, vmem, vmem),
        scratch_shapes=[
            pltpu.VMEM((side + 2, side + 2, tiles, channels), F32),
            pltpu.VMEM((side + 2, side + 2, tiles, channels), F32),
            pltpu.VMEM((side + 4, side + 4, tiles, channels), F32),
            pltpu.VMEM((side + 4, side + 4, tiles, channels), F32),
            pltpu.VMEM((side + 2, side + 2, tiles, channels), F32),
            pltpu.VMEM((side + 2, side + 2, tiles, channels), F32),
            pltpu.VMEM((side * line, channels), F32),
            pltpu.VMEM((side * line, channels), BF16),
            pltpu.VMEM((side * line, channels), BF16),
            pltpu.VMEM((edge, channels), BF16),
            pltpu.VMEM((edge + 4 * tiles, channels), BF16),
            pltpu.VMEM((edge + 4 * tiles, edge + groups * mail), BF16),
            pltpu.VMEM((groups * mail, edge), BF16),
            pltpu.VMEM((4, groups, mail, channels), BF16),
            pltpu.VMEM((4, groups, mail, channels), BF16),
            pltpu.SemaphoreType.DMA((4, groups)),
            pltpu.SemaphoreType.DMA((4, groups)),
        ],
        compiler_params=pltpu.CompilerParams(
            collective_id=0, has_side_effects=True, vmem_limit_bytes=56 * 1024 * 1024
        ),
    )(states, cotangent, beside_slot, beside_code, mixers, stencils, shifts)
    sums = lax.psum(sums, ("tile", "batch"))
    mixer_grads = sums[: 2 * channels].reshape(2, channels, channels)
    stencil_grads = sums[2 * channels : 2 * channels + 18].reshape(2, 9, channels)
    shift_grads = sums[2 * channels + 18 : 2 * channels + 20]
    return (outcome, state_grad, mixer_grads, stencil_grads, shift_grads)


def solution(mesh):
    field = P("batch", "tile", None, None, None)
    return jax.shard_map(
        shards,
        mesh=mesh,
        in_specs=(field, field, P(), P(), P(), P(), P()),
        out_specs=(field, field, P(), P(), P()),
        check_vma=False,
    )
```

time: 494 us -> 187 us (0.38); the launches traced: 484 us -> 186 us
  other arithmetic: 220 us -> 0 us
  blocking collectives: 39.6 us -> 0 us
  local copies, waits for them, and re-layouts: 48.7 us -> 9.81 us
  Pallas kernels: 0 us -> 36 us
  starting transfers between devices: 23.9 us -> 0.04 us
  matrix products: 11.9 us -> 0 us
    reduce_sum x7 -> x0, other arithmetic: 52.3 us -> none  [the longest x2 49.1 us: stencil_grad(): terms.append(jnp.sum(widened * window, axis=(0, 1, 2, 3)))]
    psum x1 -> x0, blocking collectives: 39.6 us -> none  [shards(): lax.psum((first[0], first[1], first[2], second[0], second[1], second[2]),...]
    convert_element_type x3 -> x0, other arithmetic: 39.3 us -> none  [the longest x1 19.6 us: block_pass(): conv_first = stencil_apply(padded_in, stencils[0]).astype(jnp.bfloat16)]
    mul x7 -> x0, other arithmetic: 38.7 us -> none  [the longest x2 34.6 us: stencil_back(): kernel[3 * row_at + col_at] * widened]
    pallas_call x0 -> x1, Pallas kernels: none -> 36 us  [shards(): pl.pallas_call(functools.partial(kernel, groups, scale), out_shape=(jax.S...]
    add x3 -> x0, other arithmetic: 30.6 us -> none  [the longest x2 29.5 us: stencil_back(): running + jnp.pad(kernel[3 * row_at + col_at] * widened, ((0, 0), (0, 0),...]
    scatter-add x11 -> x0, other arithmetic: 27.5 us -> none  [the longest x2 12.3 us: send_back(): rim_grad = rim_grad.at[:, own_source].add(kept_parts)]
    all_to_all x4 -> x0, starting transfers between devices: 23.8 us -> none  [the longest x2 12.3 us: send_back(): lax.all_to_all(outgoing.reshape(samples, groups, CAP, side_len, channels)...]
  transfers between devices with their start and end apart: 5 -> 1, of which waited for: 2 -> 1; matrix products, arithmetic and copies ran while one was open for 11% -> 0% of each run, Pallas kernels for 0% -> 0%
where the time goes in v1:
time: 187 us; the launch traced here: 186 us
  waiting for transfers between devices  126 us (67%)
  Pallas kernels  36 us (19%)
  between operations  14.1 us (8%)
  local copies, waits for them, and re-layouts  9.81 us (5%)
    psum x1, waiting for transfers between devices, shards(): sums = lax.psum(sums, ('tile', 'batch'))  126 us
    pallas_call x1, Pallas kernels, shards(): pl.pallas_call(functools.partial(kernel, groups, scale), out_shape=(jax.S...  36 us
    unnamed x14, local copies, waits for them, and re-layouts  5.93 us
  transfers between devices with their start and end apart: 1, of which 1 were waited for; matrix products, arithmetic and copies ran while one was open for 0% of the time, Pallas kernels for 0%

profile of v1, /device:TPU:0, one launch (start us, length us, event | category | flops | bytes accessed | tf_op | source)
XLA Modules:
  0.0 185.9 jit_solution(5040319300593999580)
XLA Ops:
  7.2 0.0 copy-start.3
  7.2 0.0 all-reduce.2.cloned.1.call-start
  7.2 1.4 copy.16.slots
  8.6 0.0 copy-done.3
  8.6 0.0 copy-start.2
  8.6 0.7 copy.17.codes
  9.3 0.0 copy-done.2
  9.3 0.6 copy.18.stencils
  10.0 36.0 %shard_map.110 = (bf16[1,8,16,16,256]{4,3,2,1,0:T(8,128)(2,1)}, bf16[1,8,16,16,256]{4,3,2,1,0:T(8,128)(2,1)}, f32[536,256]{1,0:T(8,128)}) custom-call(bf16[1,8,16,16,256]{4,3,2,1,0:T(8,128)(2,1)} %states.1, bf16[1,8,16,16,256]{4,3,2,1,0:T(8,128)(2,1)} %cotangent.1, s32[64,8]{1,0:T(8,128)} %copy.16.slots, s32[64,8]{1,0:T(8,128)} %copy.17.codes, ...), custom_call_target="tpu_custom_call" | custom-call | tf_op jit(solution)/shard_map/pallas_call | solution.py:433
  46.0 0.0 copy-start.1
  46.0 0.0 all-reduce.2.cloned.1.call-update
  46.0 126.0 %all-reduce.2.cloned.1.call-done = f32[536,256]{1,0:T(8,128)} async-done(((f32[536,256]{1,0:T(8,128)}), f32[536,256]{1,0:T(8,128)}) %all-reduce.2.cloned.1.call-update) | async-done | bytes 548880 | tf_op jit(solution)/shard_map/psum | solution.py:465
  171.9 0.7 slice.13
  172.7 0.6 copy.19
  173.3 1.9 %slice.12 = f32[512,256]{1,0:T(8,128)} slice(f32[536,256]{1,0:T(8,128)} %all-reduce.2.cloned.1.call-done), slice={[0:512], [0:256]} | slice | bytes 1048576 | tf_op jit(solution)/shard_map/slice | solution.py:466
  175.2 1.3 slice.14
  176.5 0.0 copy-done.1
  176.5 0.0 copy-start
  176.5 1.0 copy.23
  177.4 0.6 copy-done
  178.1 1.0 copy.24
  (1 shorter events, 0.0 us)
Async XLA Ops:
  7.2 1.4 copy-start.3
  7.2 164.8 %all-reduce.2.cloned.1.call-start = ((), (), s32[]{:S(2)}) async-start(), calls=%async_computation | async-start | bytes 1097728 | tf_op jit(solution)/shard_map/psum | solution.py:465
  8.6 0.7 copy-start.2
  46.0 130.5 %copy-start.1 = (bf16[1,8,16,16,256]{4,3,2,1,0:T(8,128)(2,1)S(1)}, bf16[1,8,16,16,256]{4,3,2,1,0:T(8,128)(2,1)}, u32[]{:S(2)}) copy-start(bf16[1,8,16,16,256]{4,3,2,1,0:T(8,128)(2,1)} %get-tuple-element.26) | copy-start | bytes 3145732
  176.5 1.6 copy-start
Sparse Core Ops, SparseCore 0:
  46.1 125.7 all-reduce.1

commit v2 on v1

--- a/solution.py
+++ b/solution.py
@@ -30,6 +30,7 @@
 
 def kernel(
     groups,
+    copies,
     scale,
     states,
     cotangent,
@@ -40,7 +41,13 @@
     shifts,
     outcome,
     state_grad,
+    mixer_grads,
+    stencil_grads,
+    shift_grads,
     sums,
+    shares,
+    gathered,
+    finished,
     pad_in,
     pad_mid,
     wide_second,
@@ -58,6 +65,12 @@
     inbox,
     send_sem,
     recv_sem,
+    share_send,
+    share_recv,
+    full_send,
+    full_recv,
+    slot_columns,
+    code_columns,
 ):
     tiles, side, channels = states.shape[1], states.shape[2], states.shape[4]
     line = side * tiles
@@ -71,13 +84,102 @@
 
     barrier = pltpu.get_barrier_semaphore()
 
+    devices = groups * copies
+    mine = me * copies + lax.axis_index("batch")
+
+    def other(k):
+        return lax.rem(mine + k, devices)
+
+    def place_of(device):
+        return {"tile": lax.div(device, copies), "batch": lax.rem(device, copies)}
+
     def greet(k, _):
         pl.semaphore_signal(
-            barrier, inc=1, device_id={"tile": peer_of(k)}, device_id_type=MESH
+            barrier, inc=1, device_id=place_of(other(k)), device_id_type=MESH
         )
         return 0
 
-    lax.fori_loop(1, groups, greet, 0)
+    lax.fori_loop(1, devices, greet, 0)
+
+    def share_to(x, device):
+        return pltpu.make_async_remote_copy(
+            src_ref=shares.at[x, device],
+            dst_ref=gathered.at[x, mine],
+            send_sem=share_send.at[x, device],
+            recv_sem=share_recv.at[x, mine],
+            device_id=place_of(device),
+            device_id_type=MESH,
+        )
+
+    def share_from(x, device):
+        return pltpu.make_async_remote_copy(
+            src_ref=shares.at[x, device],
+            dst_ref=gathered.at[x, device],
+            send_sem=share_send.at[x, device],
+            recv_sem=share_recv.at[x, device],
+            device_id=place_of(device),
+            device_id_type=MESH,
+        )
+
+    def full_to(x, device):
+        return pltpu.make_async_remote_copy(
+            src_ref=finished.at[x, mine],
+            dst_ref=finished.at[x, mine],
+            send_sem=full_send.at[x, device],
+            recv_sem=full_recv.at[x, mine],
+            device_id=place_of(device),
+            device_id_type=MESH,
+        )
+
+    def full_from(x, device):
+        return pltpu.make_async_remote_copy(
+            src_ref=finished.at[x, device],
+            dst_ref=finished.at[x, device],
+            send_sem=full_send.at[x, device],
+            recv_sem=full_recv.at[x, device],
+            device_id=place_of(device),
+            device_id_type=MESH,
+        )
+
+    def others(act):
+        def body(k, _):
+            act(other(k))
+            return 0
+
+        lax.fori_loop(1, devices, body, 0)
+
+    part = channels // devices
+    spare = shares.shape[2] - part
+
+    def share_out(x):
+        for device in range(devices):
+            first = x * channels + device * part
+            shares[x, device, :part] = sums[first : first + part, :]
+            if x == 1:
+                for r in range(spare):
+                    if device * spare + r < 20:
+                        row = 2 * channels + device * spare + r
+                        shares[x, device, part + r : part + r + 1] = sums[row : row + 1, :]
+        gathered[x, mine] = shares[x, mine]
+        others(lambda device: share_to(x, device).start())
+
+    def add_shares(x):
+        others(lambda device: share_from(x, device).wait_recv())
+        finished[x, mine] = jnp.sum(gathered[x], axis=0)
+        others(lambda device: full_to(x, device).start())
+
+    def take_full(x):
+        others(lambda device: full_from(x, device).wait_recv())
+        for device in range(devices):
+            mixer_grads[x, device * part : (device + 1) * part] = finished[x, device, :part]
+            if x == 1:
+                for r in range(spare):
+                    row = device * spare + r
+                    line_at = finished[x, device, part + r : part + r + 1]
+                    if row < 18:
+                        stencil_grads[row % 9, row // 9 : row // 9 + 1] = line_at
+                    elif row < 20:
+                        shift_grads[row - 18 : row - 17] = line_at
 
     def copy_to(x, peer):
         return pltpu.make_async_remote_copy(
@@ -122,10 +224,19 @@
 
     entries = 8 * tiles
 
+    count = slots.shape[1]
+    diagonal = iota((count, count), 0) == iota((count, count), 1)
+    for d in range(8):
+        for source, column in ((slots, slot_columns), (codes, code_columns)):
+            spread = jnp.broadcast_to(source[d : d + 1, :], (count, count))
+            column[:, d : d + 1] = jnp.sum(
+                jnp.where(diagonal, spread, 0), axis=1, keepdims=True
+            )
+
     def block_columns(p):
-        rows = pl.ds(p * tiles, tiles)
-        slot = slots[rows, :]
-        code = codes[rows, :]
+        rows = pl.ds(pl.multiple_of(p * tiles, tiles), tiles)
+        slot = slot_columns[rows, :]
+        code = code_columns[rows, :]
         column = lambda v: jnp.concatenate([v[:, d : d + 1] for d in range(8)], axis=0)
         slot, code = column(slot), column(code)
         owner = lax.div(slot, tiles)
@@ -241,7 +352,7 @@
                 total = None
                 for a in range(3):
                     for b in range(3):
-                        tap = stencils[layer, 3 * a + b : 3 * a + b + 1, half]
+                        tap = stencils[3 * a + b, layer : layer + 1, half]
                         term = tap[None] * pad[y + a, b : b + side, :, half]
                         total = term if total is None else total + term
                 pieces.append(total.reshape(line, total.shape[2]).astype(BF16))
@@ -256,7 +367,7 @@
                 total = None
                 for a in range(3):
                     for b in range(3):
-                        tap = stencils[layer, 3 * a + b : 3 * a + b + 1, half]
+                        tap = stencils[3 * a + b, layer : layer + 1, half]
                         term = tap[None] * wide[y + 2 - a, 2 - b : 2 - b + side + 2, :, half]
                         total = term if total is None else total + term
                 out[y, :, :, half] = total
@@ -315,8 +426,10 @@
     step = max(s for s in (1, 2, 4) if side % s == 0)
     chunk = step * line
 
-    pl.semaphore_wait(barrier, groups - 1)
+    pl.semaphore_wait(barrier, devices - 1)
     post_rims(0, pad_in)
+
+    shares[...] = jnp.zeros(shares.shape, F32)
 
     def take_cotangent(c, total):
         for r in range(step):
@@ -324,8 +437,8 @@
             x = dot(turn, cotangent[0, :, y].reshape(line, channels))
             total = total + jnp.sum(x.reshape(side, tiles, channels), axis=0)
             cot[pl.ds(pl.multiple_of(y * line, line), line), :] = x.astype(BF16)
-        mine = cot[pl.ds(pl.multiple_of(c * chunk, chunk), chunk), :]
-        grad = dot(mine, mixers[1], 1, 1).astype(BF16).astype(F32)
+        piece = cot[pl.ds(pl.multiple_of(c * chunk, chunk), chunk), :]
+        grad = dot(piece, mixers[1], 1, 1).astype(BF16).astype(F32)
         wide_second[pl.ds(c * step + 2, step), 2 : side + 2] = grad.reshape(
             step, side, tiles, channels
         )
@@ -334,7 +447,6 @@
     total = lax.fori_loop(0, side // step, take_cotangent, jnp.zeros((tiles, channels), F32))
     row = extra + 19
     sums[row : row + 1, :] = jnp.sum(total, axis=0, keepdims=True) * scale
-    sums[row + 1 :, :] = jnp.zeros((sums.shape[0] - row - 1, channels), F32)
 
     convolve_back(wide_second, back_second, 1)
     post_parts(1, back_second)
@@ -382,19 +494,28 @@
 
     convolve_back(wide_first, back_first, 0)
     post_parts(3, back_first)
+    share_out(0)
     add_local(back_first)
     stencil_sums(wide_first, pad_in, 0)
 
     receive(2)
     fill_halo(2, pad_mid)
     convolve(pad_mid, 1)
-    stencil_sums(wide_second, pad_mid, 1)
-
-    def mix_second(c, _):
+
+    def grad_mixer(c, _):
         rows = pl.ds(pl.multiple_of(c * chunk, chunk), chunk)
         sums[channels : 2 * channels, :] = (
             sums[channels : 2 * channels, :] + dot(conv[rows, :], cot[rows, :], 0, 0) * scale
         )
+        return 0
+
+    lax.fori_loop(0, side // step, grad_mixer, 0)
+    stencil_sums(wide_second, pad_mid, 1)
+    share_out(1)
+    add_shares(0)
+
+    def mix_second(c, _):
+        rows = pl.ds(pl.multiple_of(c * chunk, chunk), chunk)
         held = pad_in[pl.ds(c * step + 1, step), 1 : side + 1].reshape(chunk, channels)
         result = (held + dot(conv[rows, :], mixers[1]) + shifts[1:2, :]).astype(BF16)
         for r in range(step):
@@ -416,30 +537,47 @@
         return 0
 
     lax.fori_loop(0, side, put_grad, 0)
+    add_shares(1)
+    take_full(0)
     for x in range(4):
         finish_sends(x)
+    for x in range(2):
+        others(lambda device: share_to(x, device).wait_send())
+    take_full(1)
+    for x in range(2):
+        others(lambda device: full_to(x, device).wait_send())
 
 
 def shards(states, cotangent, beside_slot, beside_code, mixers, stencils, shifts):
     samples, tiles, side, _, channels = states.shape
     groups = lax.axis_size("tile")
-    total = samples * tiles * side * side * groups * lax.axis_size("batch")
+    copies = lax.axis_size("batch")
+    devices = groups * copies
+    part = channels // devices
+    spare = -(-20 // devices)
+    total = samples * tiles * side * side * devices
     scale = 1.0 / math.sqrt(total)
     rows = -(-(2 * channels + 20) // 8) * 8
     line = side * tiles
     edge = 4 * line
     mail = CAP * side
     vmem = pl.BlockSpec(memory_space=pltpu.VMEM)
-    outcome, state_grad, sums = pl.pallas_call(
-        functools.partial(kernel, groups, scale),
+    outcome, state_grad, mixer_grads, stencil_grads, shift_grads = pl.pallas_call(
+        functools.partial(kernel, groups, copies, scale),
         out_shape=(
             jax.ShapeDtypeStruct(states.shape, BF16),
             jax.ShapeDtypeStruct(states.shape, BF16),
-            jax.ShapeDtypeStruct((rows, channels), F32),
+            jax.ShapeDtypeStruct(mixers.shape, F32),
+            jax.ShapeDtypeStruct((9, 2, channels), F32),
+            jax.ShapeDtypeStruct(shifts.shape, F32),
         ),
         in_specs=[vmem] * 7,
-        out_specs=(vmem, vmem, vmem),
+        out_specs=(vmem,) * 5,
         scratch_shapes=[
+            pltpu.VMEM((rows, channels), F32),
+            pltpu.VMEM((2, devices, part + spare, channels), F32),
+            pltpu.VMEM((2, devices, part + spare, channels), F32),
+            pltpu.VMEM((2, devices, part + spare, channels), F32),
             pltpu.VMEM((side + 2, side + 2, tiles, channels), F32),
             pltpu.VMEM((side + 2, side + 2, tiles, channels), F32),
             pltpu.VMEM((side + 4, side + 4, tiles, channels), F32),
@@ -457,16 +595,26 @@
             pltpu.VMEM((4, groups, mail, channels), BF16),
             pltpu.SemaphoreType.DMA((4, groups)),
             pltpu.SemaphoreType.DMA((4, groups)),
+            pltpu.SemaphoreType.DMA((2, devices)),
+            pltpu.SemaphoreType.DMA((2, devices)),
+            pltpu.SemaphoreType.DMA((2, devices)),
+            pltpu.SemaphoreType.DMA((2, devices)),
+            pltpu.VMEM(beside_slot.shape, jnp.int32),
+            pltpu.VMEM(beside_code.shape, jnp.int32),
         ],
         compiler_params=pltpu.CompilerParams(
             collective_id=0, has_side_effects=True, vmem_limit_bytes=56 * 1024 * 1024
         ),
-    )(states, cotangent, beside_slot, beside_code, mixers, stencils, shifts)
-    sums = lax.psum(sums, ("tile", "batch"))
-    mixer_grads = sums[: 2 * channels].reshape(2, channels, channels)
-    stencil_grads = sums[2 * channels : 2 * channels + 18].reshape(2, 9, channels)
-    shift_grads = sums[2 * channels + 18 : 2 * channels + 20]
-    return (outcome, state_grad, mixer_grads, stencil_grads, shift_grads)
+    )(
+        states,
+        cotangent,
+        beside_slot.T,
+        beside_code.T,
+        mixers,
+        stencils.transpose(1, 0, 2),
+        shifts,
+    )
+    return (outcome, state_grad, mixer_grads, stencil_grads.transpose(1, 0, 2), shift_grads)
 
 
 def solution(mesh):

time: 187 us -> 83 us (0.44)
  waiting for transfers between devices: 126 us -> 0 us
  Pallas kernels: 36 us -> 75.4 us
  between operations: 14.1 us -> 0.66 us
  local copies, waits for them, and re-layouts: 9.81 us -> 5.8 us
    psum x1 -> x0, waiting for transfers between devices: 126 us -> none  [shards(): sums = lax.psum(sums, ('tile', 'batch'))]
    pallas_call x1, Pallas kernels: 36 us -> 75.4 us  [shards(): pl.pallas_call(functools.partial(kernel, groups, copies, scale), out_shap...]
    slice x3 -> x0, local copies, waits for them, and re-layouts: 3.88 us -> none  [the longest x1 1.87 us: shards(): mixer_grads = sums[:2 * channels].reshape(2, channels, channels)]
    unnamed x14 -> x13, local copies, waits for them, and re-layouts: 5.93 us -> 5.8 us
  transfers between devices with their start and end apart: 1 -> 0, of which waited for: 1 -> 0; matrix products, arithmetic and copies ran while one was open for 0% -> 0% of each run, Pallas kernels for 0% -> 0%
where the time goes in v2:
time: 83 us; the launch traced here: 81.9 us
  Pallas kernels  75.4 us (91%)
  local copies, waits for them, and re-layouts  5.8 us (7%)
    pallas_call x1, Pallas kernels, shards(): pl.pallas_call(functools.partial(kernel, groups, copies, scale), out_shap...  75.4 us
    unnamed x13, local copies, waits for them, and re-layouts  5.8 us

profile of v2, /device:TPU:0, one launch (start us, length us, event | category | flops | bytes accessed | tf_op | source)
XLA Modules:
  0.0 81.9 jit_solution(2856775014138879721)
XLA Ops:
  0.6 75.4 %shard_map.110 = (bf16[1,8,16,16,256]{4,3,2,1,0:T(8,128)(2,1)}, bf16[1,8,16,16,256]{4,3,2,1,0:T(8,128)(2,1)}, f32[2,256,256]{2,1,0:T(8,128)}, f32[9,2,256]{2,1,0:T(2,128)}, f32[2,256]{1,0:T(2,128)}) custom-call(bf16[1,8,16,16,256]{4,3,2,1,0:T(8,128)(2,1)} %states.1, bf16[1,8,16,16,256]{4,3,2,1,0:T(8,128)(2,1)} %cotangent.1, s32[8,64]{1,0:T(8,128)} %bitcast.6, ...), custom_call_target="tpu_custom_call" | custom-call | tf_op jit(solution)/shard_map/pallas_call | solution.py:565
  76.0 0.0 copy-start
  76.1 2.4 %copy.17 = bf16[1,8,16,16,256]{4,3,2,1,0:T(8,128)(2,1)} copy(bf16[1,8,16,16,256]{4,3,2,1,0:T(8,128)(2,1)} %get-tuple-element.20) | data formatting | bytes 2097152
  78.4 0.0 copy-done
  78.4 0.0 copy-start.1
  78.4 1.0 %copy.18 = bf16[1,8,16,16,256]{4,3,2,1,0:T(8,128)(2,1)} copy(bf16[1,8,16,16,256]{4,3,2,1,0:T(8,128)(2,1)S(1)} %copy-done) | data formatting | bytes 2097152
  79.4 0.4 copy-done.1
  79.8 0.0 copy-start.2
  79.8 0.8 copy.19
  80.6 0.0 copy-done.2
  80.6 0.0 copy-start.3
  80.6 0.6 copy.20
  81.2 0.1 copy-done.3
  81.3 0.6 copy.21
Async XLA Ops:
  76.0 2.4 %copy-start = (bf16[1,8,16,16,256]{4,3,2,1,0:T(8,128)(2,1)S(1)}, bf16[1,8,16,16,256]{4,3,2,1,0:T(8,128)(2,1)}, u32[]{:S(2)}) copy-start(bf16[1,8,16,16,256]{4,3,2,1,0:T(8,128)(2,1)} %get-tuple-element.21) | copy-start | bytes 3145732
  78.4 1.4 %copy-start.1 = (f32[2,256,256]{2,1,0:T(8,128)S(1)}, f32[2,256,256]{2,1,0:T(8,128)}, u32[]{:S(2)}) copy-start(f32[2,256,256]{2,1,0:T(8,128)} %get-tuple-element.22) | copy-start | bytes 1572868
  79.8 0.8 copy-start.2
  80.6 0.7 copy-start.3

commit v3 on v1

--- a/solution.py
+++ b/solution.py
@@ -30,6 +30,7 @@
 
 def kernel(
     groups,
+    copies,
     scale,
     states,
     cotangent,
@@ -40,25 +41,36 @@
     shifts,
     outcome,
     state_grad,
+    mixer_grads,
+    stencil_grads,
+    shift_grads,
     sums,
-    pad_in,
-    pad_mid,
-    wide_second,
-    wide_first,
-    back_second,
-    back_first,
-    slope,
-    conv,
-    cot,
-    rims,
-    parts,
-    fetch_map,
-    send_map,
-    outbox,
-    inbox,
-    send_sem,
-    recv_sem,
+    *scratch,
 ):
+    (
+        pad_in,
+        pad_mid,
+        wide_second,
+        wide_first,
+        back_second,
+        back_first,
+        slope,
+        conv,
+        cot,
+        rims,
+        parts,
+        fetch_map,
+        send_map,
+        outbox,
+        inbox,
+        send_sem,
+        recv_sem,
+        slot_columns,
+        code_columns,
+    ) = scratch[:19]
+    staged = scratch[19:]
+    shares, near, middle, far, finished = (staged[3 * k : 3 * k + 3] for k in range(5))
+    stage_send, stage_recv = staged[15:19], staged[19:23]
     tiles, side, channels = states.shape[1], states.shape[2], states.shape[4]
     line = side * tiles
     edge = 4 * line
@@ -71,13 +83,117 @@
 
     barrier = pltpu.get_barrier_semaphore()
 
-    def greet(k, _):
-        pl.semaphore_signal(
-            barrier, inc=1, device_id={"tile": peer_of(k)}, device_id_type=MESH
-        )
-        return 0
-
-    lax.fori_loop(1, groups, greet, 0)
+    devices = groups * copies
+    twin = lax.axis_index("batch")
+    rings = {"tile": (me, groups), "batch": (twin, copies)}
+
+    def others(axis, act):
+        at, size = rings[axis]
+
+        def body(k, _):
+            act(lax.rem(at + k, size))
+            return 0
+
+        lax.fori_loop(1, size, body, 0)
+
+    for axis in rings:
+        others(
+            axis,
+            lambda peer, axis=axis: pl.semaphore_signal(
+                barrier, inc=1, device_id={axis: peer}, device_id_type=MESH
+            ),
+        )
+
+    part = channels // devices
+    spare = -(-20 // devices)
+
+    def rdma(axis, peer, stage, x, src, dst, slot):
+        return pltpu.make_async_remote_copy(
+            src_ref=src,
+            dst_ref=dst,
+            send_sem=stage_send[stage].at[x, peer],
+            recv_sem=stage_recv[stage].at[x, slot],
+            device_id={axis: peer},
+            device_id_type=MESH,
+        )
+
+    def scatter_batch(x, peer, slot):
+        return rdma("batch", peer, 0, x, shares[x].at[peer], near[x].at[slot], slot)
+
+    def scatter_tile(x, peer, slot):
+        return rdma("tile", peer, 1, x, middle[x].at[peer], far[x].at[slot], slot)
+
+    def gather_tile(x, peer, slot):
+        place = finished[x].at[twin, slot]
+        return rdma("tile", peer, 2, x, place, place, slot)
+
+    def gather_batch(x, peer, slot):
+        place = finished[x].at[slot]
+        return rdma("batch", peer, 3, x, place, place, slot)
+
+    def start(make, axis, x):
+        at = rings[axis][0]
+        others(axis, lambda peer: make(x, peer, at).start())
+
+    def arrive(make, axis, x):
+        others(axis, lambda peer: make(x, peer, peer).wait_recv())
+
+    def leave(make, axis, x):
+        at = rings[axis][0]
+        others(axis, lambda peer: make(x, peer, at).wait_send())
+
+    def stage_one(x):
+        for b in range(copies):
+            for g in range(groups):
+                order = b * groups + g
+                if x < 2:
+                    first = x * channels + order * part
+                    shares[x][b, g] = sums[first : first + part, :]
+                else:
+                    for r in range(spare):
+                        row = order * spare + r
+                        if row < 20:
+                            row_at = 2 * channels + row
+                            shares[x][b, g, r : r + 1] = sums[row_at : row_at + 1, :]
+        near[x][twin] = shares[x][twin]
+        start(scatter_batch, "batch", x)
+
+    def stage_two(x):
+        arrive(scatter_batch, "batch", x)
+        middle[x][...] = jnp.sum(near[x][...], axis=0)
+        far[x][me] = middle[x][me]
+        start(scatter_tile, "tile", x)
+
+    def stage_three(x):
+        arrive(scatter_tile, "tile", x)
+        finished[x][twin, me] = jnp.sum(far[x][...], axis=0)
+        start(gather_tile, "tile", x)
+
+    def stage_four(x):
+        arrive(gather_tile, "tile", x)
+        start(gather_batch, "batch", x)
+
+    def stage_last(x):
+        arrive(gather_batch, "batch", x)
+        for b in range(copies):
+            for g in range(groups):
+                order = b * groups + g
+                if x < 2:
+                    mixer_grads[x, order * part : (order + 1) * part] = finished[x][b, g]
+                else:
+                    for r in range(spare):
+                        row = order * spare + r
+                        line_at = finished[x][b, g, r : r + 1]
+                        if row < 18:
+                            stencil_grads[row % 9, row // 9 : row // 9 + 1] = line_at
+                        elif row < 20:
+                            shift_grads[row - 18 : row - 17] = line_at
+
+    def stage_waits(x):
+        leave(scatter_batch, "batch", x)
+        leave(scatter_tile, "tile", x)
+        leave(gather_tile, "tile", x)
+        leave(gather_batch, "batch", x)
 
     def copy_to(x, peer):
         return pltpu.make_async_remote_copy(
@@ -122,10 +238,19 @@
 
     entries = 8 * tiles
 
+    count = slots.shape[1]
+    diagonal = iota((count, count), 0) == iota((count, count), 1)
+    for d in range(8):
+        for source, column in ((slots, slot_columns), (codes, code_columns)):
+            spread = jnp.broadcast_to(source[d : d + 1, :], (count, count))
+            column[:, d : d + 1] = jnp.sum(
+                jnp.where(diagonal, spread, 0), axis=1, keepdims=True
+            )
+
     def block_columns(p):
-        rows = pl.ds(p * tiles, tiles)
-        slot = slots[rows, :]
-        code = codes[rows, :]
+        rows = pl.ds(pl.multiple_of(p * tiles, tiles), tiles)
+        slot = slot_columns[rows, :]
+        code = code_columns[rows, :]
         column = lambda v: jnp.concatenate([v[:, d : d + 1] for d in range(8)], axis=0)
         slot, code = column(slot), column(code)
         owner = lax.div(slot, tiles)
@@ -241,7 +366,7 @@
                 total = None
                 for a in range(3):
                     for b in range(3):
-                        tap = stencils[layer, 3 * a + b : 3 * a + b + 1, half]
+                        tap = stencils[3 * a + b, layer : layer + 1, half]
                         term = tap[None] * pad[y + a, b : b + side, :, half]
                         total = term if total is None else total + term
                 pieces.append(total.reshape(line, total.shape[2]).astype(BF16))
@@ -256,7 +381,7 @@
                 total = None
                 for a in range(3):
                     for b in range(3):
-                        tap = stencils[layer, 3 * a + b : 3 * a + b + 1, half]
+                        tap = stencils[3 * a + b, layer : layer + 1, half]
                         term = tap[None] * wide[y + 2 - a, 2 - b : 2 - b + side + 2, :, half]
                         total = term if total is None else total + term
                 out[y, :, :, half] = total
@@ -315,8 +440,10 @@
     step = max(s for s in (1, 2, 4) if side % s == 0)
     chunk = step * line
 
-    pl.semaphore_wait(barrier, groups - 1)
+    pl.semaphore_wait(barrier, groups + copies - 2)
     post_rims(0, pad_in)
+
+    shares[2][...] = jnp.zeros(shares[2].shape, F32)
 
     def take_cotangent(c, total):
         for r in range(step):
@@ -324,8 +451,8 @@
             x = dot(turn, cotangent[0, :, y].reshape(line, channels))
             total = total + jnp.sum(x.reshape(side, tiles, channels), axis=0)
             cot[pl.ds(pl.multiple_of(y * line, line), line), :] = x.astype(BF16)
-        mine = cot[pl.ds(pl.multiple_of(c * chunk, chunk), chunk), :]
-        grad = dot(mine, mixers[1], 1, 1).astype(BF16).astype(F32)
+        piece = cot[pl.ds(pl.multiple_of(c * chunk, chunk), chunk), :]
+        grad = dot(piece, mixers[1], 1, 1).astype(BF16).astype(F32)
         wide_second[pl.ds(c * step + 2, step), 2 : side + 2] = grad.reshape(
             step, side, tiles, channels
         )
@@ -334,7 +461,6 @@
     total = lax.fori_loop(0, side // step, take_cotangent, jnp.zeros((tiles, channels), F32))
     row = extra + 19
     sums[row : row + 1, :] = jnp.sum(total, axis=0, keepdims=True) * scale
-    sums[row + 1 :, :] = jnp.zeros((sums.shape[0] - row - 1, channels), F32)
 
     convolve_back(wide_second, back_second, 1)
     post_parts(1, back_second)
@@ -382,19 +508,31 @@
 
     convolve_back(wide_first, back_first, 0)
     post_parts(3, back_first)
+    stage_one(0)
     add_local(back_first)
-    stencil_sums(wide_first, pad_in, 0)
 
     receive(2)
     fill_halo(2, pad_mid)
     convolve(pad_mid, 1)
-    stencil_sums(wide_second, pad_mid, 1)
-
-    def mix_second(c, _):
+    stage_two(0)
+
+    def grad_mixer(c, _):
         rows = pl.ds(pl.multiple_of(c * chunk, chunk), chunk)
         sums[channels : 2 * channels, :] = (
             sums[channels : 2 * channels, :] + dot(conv[rows, :], cot[rows, :], 0, 0) * scale
         )
+        return 0
+
+    lax.fori_loop(0, side // step, grad_mixer, 0)
+    stage_one(1)
+    stencil_sums(wide_second, pad_mid, 1)
+    stage_three(0)
+    stencil_sums(wide_first, pad_in, 0)
+    stage_one(2)
+    stage_two(1)
+
+    def mix_second(c, _):
+        rows = pl.ds(pl.multiple_of(c * chunk, chunk), chunk)
         held = pad_in[pl.ds(c * step + 1, step), 1 : side + 1].reshape(chunk, channels)
         result = (held + dot(conv[rows, :], mixers[1]) + shifts[1:2, :]).astype(BF16)
         for r in range(step):
@@ -403,6 +541,9 @@
         return 0
 
     lax.fori_loop(0, side // step, mix_second, 0)
+    stage_four(0)
+    stage_two(2)
+    stage_three(1)
 
     receive(3)
     add_remote(3, back_first)
@@ -416,30 +557,52 @@
         return 0
 
     lax.fori_loop(0, side, put_grad, 0)
+    stage_three(2)
+    stage_four(1)
+    stage_four(2)
+    stage_last(0)
     for x in range(4):
         finish_sends(x)
+    stage_last(1)
+    stage_last(2)
+    for x in range(3):
+        stage_waits(x)
 
 
 def shards(states, cotangent, beside_slot, beside_code, mixers, stencils, shifts):
     samples, tiles, side, _, channels = states.shape
     groups = lax.axis_size("tile")
-    total = samples * tiles * side * side * groups * lax.axis_size("batch")
+    copies = lax.axis_size("batch")
+    devices = groups * copies
+    part = channels // devices
+    spare = -(-20 // devices)
+    total = samples * tiles * side * side * devices
     scale = 1.0 / math.sqrt(total)
     rows = -(-(2 * channels + 20) // 8) * 8
     line = side * tiles
     edge = 4 * line
     mail = CAP * side
     vmem = pl.BlockSpec(memory_space=pltpu.VMEM)
-    outcome, state_grad, sums = pl.pallas_call(
-        functools.partial(kernel, groups, scale),
+    heights = (part, part, spare)
+    stages = []
+    for lead in ((copies, groups), (copies, groups), (groups,), (groups,), (copies, groups)):
+        stages += [pltpu.VMEM(lead + (height, channels), F32) for height in heights]
+    for _ in range(2):
+        for size in (copies, groups, groups, copies):
+            stages.append(pltpu.SemaphoreType.DMA((3, size)))
+    outcome, state_grad, mixer_grads, stencil_grads, shift_grads = pl.pallas_call(
+        functools.partial(kernel, groups, copies, scale),
         out_shape=(
             jax.ShapeDtypeStruct(states.shape, BF16),
             jax.ShapeDtypeStruct(states.shape, BF16),
-            jax.ShapeDtypeStruct((rows, channels), F32),
+            jax.ShapeDtypeStruct(mixers.shape, F32),
+            jax.ShapeDtypeStruct((9, 2, channels), F32),
+            jax.ShapeDtypeStruct(shifts.shape, F32),
         ),
         in_specs=[vmem] * 7,
-        out_specs=(vmem, vmem, vmem),
+        out_specs=(vmem,) * 5,
         scratch_shapes=[
+            pltpu.VMEM((rows, channels), F32),
             pltpu.VMEM((side + 2, side + 2, tiles, channels), F32),
             pltpu.VMEM((side + 2, side + 2, tiles, channels), F32),
             pltpu.VMEM((side + 4, side + 4, tiles, channels), F32),
@@ -457,16 +620,23 @@
             pltpu.VMEM((4, groups, mail, channels), BF16),
             pltpu.SemaphoreType.DMA((4, groups)),
             pltpu.SemaphoreType.DMA((4, groups)),
+            pltpu.VMEM(beside_slot.shape, jnp.int32),
+            pltpu.VMEM(beside_code.shape, jnp.int32),
+            *stages,
         ],
         compiler_params=pltpu.CompilerParams(
             collective_id=0, has_side_effects=True, vmem_limit_bytes=56 * 1024 * 1024
         ),
-    )(states, cotangent, beside_slot, beside_code, mixers, stencils, shifts)
-    sums = lax.psum(sums, ("tile", "batch"))
-    mixer_grads = sums[: 2 * channels].reshape(2, channels, channels)
-    stencil_grads = sums[2 * channels : 2 * channels + 18].reshape(2, 9, channels)
-    shift_grads = sums[2 * channels + 18 : 2 * channels + 20]
-    return (outcome, state_grad, mixer_grads, stencil_grads, shift_grads)
+    )(
+        states,
+        cotangent,
+        beside_slot.T,
+        beside_code.T,
+        mixers,
+        stencils.transpose(1, 0, 2),
+        shifts,
+    )
+    return (outcome, state_grad, mixer_grads, stencil_grads.transpose(1, 0, 2), shift_grads)
 
 
 def solution(mesh):

time: 187 us -> 58.6 us (0.31)
  waiting for transfers between devices: 126 us -> 0 us
  Pallas kernels: 36 us -> 51.9 us
  between operations: 14.1 us -> 0.66 us
  local copies, waits for them, and re-layouts: 9.81 us -> 5.8 us
    psum x1 -> x0, waiting for transfers between devices: 126 us -> none  [shards(): sums = lax.psum(sums, ('tile', 'batch'))]
    pallas_call x1, Pallas kernels: 36 us -> 51.9 us  [shards(): pl.pallas_call(functools.partial(kernel, groups, copies, scale), out_shap...]
    slice x3 -> x0, local copies, waits for them, and re-layouts: 3.88 us -> none  [the longest x1 1.87 us: shards(): mixer_grads = sums[:2 * channels].reshape(2, channels, channels)]
    unnamed x14 -> x13, local copies, waits for them, and re-layouts: 5.93 us -> 5.8 us
  transfers between devices with their start and end apart: 1 -> 0, of which waited for: 1 -> 0; matrix products, arithmetic and copies ran while one was open for 0% -> 0% of each run, Pallas kernels for 0% -> 0%
where the time goes in v3:
time: 58.6 us; the launch traced here: 58.3 us
  Pallas kernels  51.9 us (89%)
  local copies, waits for them, and re-layouts  5.8 us (10%)
  between operations  0.66 us (1%)
    pallas_call x1, Pallas kernels, shards(): pl.pallas_call(functools.partial(kernel, groups, copies, scale), out_shap...  51.9 us
    unnamed x13, local copies, waits for them, and re-layouts  5.8 us

profile of v3, /device:TPU:0, one launch (start us, length us, event | category | flops | bytes accessed | tf_op | source)
XLA Modules:
  0.0 58.3 jit_solution(16047984564157404344)
XLA Ops:
  0.6 51.9 %shard_map.110 = (bf16[1,8,16,16,256]{4,3,2,1,0:T(8,128)(2,1)}, bf16[1,8,16,16,256]{4,3,2,1,0:T(8,128)(2,1)}, f32[2,256,256]{2,1,0:T(8,128)}, f32[9,2,256]{2,1,0:T(2,128)}, f32[2,256]{1,0:T(2,128)}) custom-call(bf16[1,8,16,16,256]{4,3,2,1,0:T(8,128)(2,1)} %states.1, bf16[1,8,16,16,256]{4,3,2,1,0:T(8,128)(2,1)} %cotangent.1, s32[8,64]{1,0:T(8,128)} %bitcast.6, ...), custom_call_target="tpu_custom_call" | custom-call | tf_op jit(solution)/shard_map/pallas_call | solution.py:593
  52.5 0.0 copy-start
  52.5 2.4 %copy.17 = bf16[1,8,16,16,256]{4,3,2,1,0:T(8,128)(2,1)} copy(bf16[1,8,16,16,256]{4,3,2,1,0:T(8,128)(2,1)} %get-tuple-element.20) | data formatting | bytes 2097152
  54.9 0.0 copy-done
  54.9 0.0 copy-start.1
  54.9 1.0 %copy.18 = bf16[1,8,16,16,256]{4,3,2,1,0:T(8,128)(2,1)} copy(bf16[1,8,16,16,256]{4,3,2,1,0:T(8,128)(2,1)S(1)} %copy-done) | data formatting | bytes 2097152
  55.8 0.4 copy-done.1
  56.3 0.0 copy-start.2
  56.3 0.8 %copy.19 = f32[2,256,256]{2,1,0:T(8,128)} copy(f32[2,256,256]{2,1,0:T(8,128)S(1)} %copy-done.1) | data formatting | bytes 1048576
  57.1 0.0 copy-done.2
  57.1 0.0 copy-start.3
  57.1 0.6 %copy.20 = f32[2,9,256]{2,0,1:T(2,128)} copy(f32[2,9,256]{2,0,1:T(2,128)S(1)} %bitcast.5) | data formatting | bytes 36864
  57.7 0.1 copy-done.3
  57.7 0.6 copy.21
Async XLA Ops:
  52.5 2.4 %copy-start = (bf16[1,8,16,16,256]{4,3,2,1,0:T(8,128)(2,1)S(1)}, bf16[1,8,16,16,256]{4,3,2,1,0:T(8,128)(2,1)}, u32[]{:S(2)}) copy-start(bf16[1,8,16,16,256]{4,3,2,1,0:T(8,128)(2,1)} %get-tuple-element.21) | copy-start | bytes 3145732
  54.9 1.4 %copy-start.1 = (f32[2,256,256]{2,1,0:T(8,128)S(1)}, f32[2,256,256]{2,1,0:T(8,128)}, u32[]{:S(2)}) copy-start(f32[2,256,256]{2,1,0:T(8,128)} %get-tuple-element.22) | copy-start | bytes 1572868
  56.3 0.8 %copy-start.2 = (f32[9,2,256]{2,1,0:T(2,128)S(1)}, f32[9,2,256]{2,1,0:T(2,128)}, u32[]{:S(2)}) copy-start(f32[9,2,256]{2,1,0:T(2,128)} %get-tuple-element.13) | copy-start | bytes 55300
  57.1 0.7 %copy-start.3 = (f32[2,256]{1,0:T(2,128)S(1)}, f32[2,256]{1,0:T(2,128)}, u32[]{:S(2)}) copy-start(f32[2,256]{1,0:T(2,128)} %get-tuple-element.24) | copy-start | bytes 6148

commit v4 on v3

--- a/solution.py
+++ b/solution.py
@@ -321,12 +321,16 @@
             wide[rows] = jnp.zeros((2, side + 4, tiles, channels), F32)
             wide[2 : side + 2, rows] = jnp.zeros((side, 2, tiles, channels), F32)
 
-    def take_states(y, _):
-        x = states[0, :, y].reshape(line, channels)
-        pad_in[y + 1, 1 : side + 1] = dot(turn, x).reshape(side, tiles, channels)
+    step = max(s for s in (1, 2, 4) if side % s == 0)
+    chunk = step * line
+
+    def take_states(c, _):
+        for r in range(step):
+            x = states[0, :, c * step + r].reshape(line, channels)
+            pad_in[c * step + r + 1, 1 : side + 1] = dot(turn, x).reshape(side, tiles, channels)
         return 0
 
-    lax.fori_loop(0, side, take_states, 0)
+    lax.fori_loop(0, side // step, take_states, 0)
 
     def take_rims(pad):
         inner = slice(1, side + 1)
@@ -437,9 +441,6 @@
     def add_remote(x, back):
         add_rims(back, dot(send_map[...], inbox[x].reshape(groups * mail, channels), 0, 0))
 
-    step = max(s for s in (1, 2, 4) if side % s == 0)
-    chunk = step * line
-
     pl.semaphore_wait(barrier, groups + copies - 2)
     post_rims(0, pad_in)
 
@@ -510,6 +511,7 @@
     post_parts(3, back_first)
     stage_one(0)
     add_local(back_first)
+    stencil_sums(wide_first, pad_in, 0)
 
     receive(2)
     fill_halo(2, pad_mid)
@@ -526,10 +528,10 @@
     lax.fori_loop(0, side // step, grad_mixer, 0)
     stage_one(1)
     stencil_sums(wide_second, pad_mid, 1)
+    stage_one(2)
     stage_three(0)
-    stencil_sums(wide_first, pad_in, 0)
-    stage_one(2)
     stage_two(1)
+    half_way = side // step // 2
 
     def mix_second(c, _):
         rows = pl.ds(pl.multiple_of(c * chunk, chunk), chunk)
@@ -540,26 +542,30 @@
             outcome[0, :, c * step + r] = turned.astype(BF16).reshape(tiles, side, channels)
         return 0
 
-    lax.fori_loop(0, side // step, mix_second, 0)
+    lax.fori_loop(0, half_way, mix_second, 0)
+    stage_two(2)
     stage_four(0)
-    stage_two(2)
+    lax.fori_loop(half_way, side // step, mix_second, 0)
     stage_three(1)
+    stage_three(2)
 
     receive(3)
     add_remote(3, back_first)
 
-    def put_grad(y, _):
-        inner = back_first[y + 1, 1 : side + 1].reshape(line, channels)
-        rows = pl.ds(pl.multiple_of(y * line, line), line)
-        result = (cot[rows, :].astype(F32) + inner).astype(BF16)
-        turned = dot(turn_back, result)
-        state_grad[0, :, y] = turned.astype(BF16).reshape(tiles, side, channels)
+    def put_grad(c, _):
+        for r in range(step):
+            y = c * step + r
+            inner = back_first[y + 1, 1 : side + 1].reshape(line, channels)
+            rows = pl.ds(pl.multiple_of(y * line, line), line)
+            result = (cot[rows, :].astype(F32) + inner).astype(BF16)
+            turned = dot(turn_back, result)
+            state_grad[0, :, y] = turned.astype(BF16).reshape(tiles, side, channels)
         return 0
 
-    lax.fori_loop(0, side, put_grad, 0)
-    stage_three(2)
+    lax.fori_loop(0, half_way, put_grad, 0)
     stage_four(1)
     stage_four(2)
+    lax.fori_loop(half_way, side // step, put_grad, 0)
     stage_last(0)
     for x in range(4):
         finish_sends(x)
@@ -567,6 +573,15 @@
     stage_last(2)
     for x in range(3):
         stage_waits(x)
+
+
+def hand_on(*refs):
+    sources, targets, sems = refs[:5], refs[5:10], refs[10]
+    moves = [pltpu.make_async_copy(sources[k], targets[k], sems.at[k]) for k in range(5)]
+    for move in moves:
+        move.start()
+    for move in moves:
+        move.wait()
 
 
 def shards(states, cotangent, beside_slot, beside_code, mixers, stencils, shifts):
@@ -590,7 +605,7 @@
     for _ in range(2):
         for size in (copies, groups, groups, copies):
             stages.append(pltpu.SemaphoreType.DMA((3, size)))
-    outcome, state_grad, mixer_grads, stencil_grads, shift_grads = pl.pallas_call(
+    results = pl.pallas_call(
         functools.partial(kernel, groups, copies, scale),
         out_shape=(
             jax.ShapeDtypeStruct(states.shape, BF16),
@@ -636,6 +651,15 @@
         stencils.transpose(1, 0, 2),
         shifts,
     )
+    anywhere = pl.BlockSpec(memory_space=pl.ANY)
+    outcome, state_grad, mixer_grads, stencil_grads, shift_grads = pl.pallas_call(
+        hand_on,
+        out_shape=[jax.ShapeDtypeStruct(r.shape, r.dtype) for r in results],
+        in_specs=[anywhere] * 5,
+        out_specs=[anywhere] * 5,
+        scratch_shapes=[pltpu.SemaphoreType.DMA((5,))],
+        compiler_params=pltpu.CompilerParams(vmem_limit_bytes=56 * 1024 * 1024),
+    )(*results)
     return (outcome, state_grad, mixer_grads, stencil_grads.transpose(1, 0, 2), shift_grads)
 
 

time: 58.6 us -> 131 us (2.24)
  Pallas kernels: 51.9 us -> 130 us
  local copies, waits for them, and re-layouts: 5.8 us -> 0 us
    pallas_call x0 -> x1, Pallas kernels: none -> 81.2 us  [shards(): pl.pallas_call(hand_on, out_shape=[jax.ShapeDtypeStruct(r.shape, r.dtype)...]
    unnamed x13 -> x0, local copies, waits for them, and re-layouts: 5.8 us -> none
    pallas_call x1, Pallas kernels: 51.9 us -> 49 us  [shards(): pl.pallas_call(functools.partial(kernel, groups, copies, scale), out_shap...]
where the time goes in v4:
time: 131 us
  Pallas kernels  130 us (99%)
    pallas_call x1, Pallas kernels, shards(): pl.pallas_call(hand_on, out_shape=[jax.ShapeDtypeStruct(r.shape, r.dtype)...  81.2 us
    pallas_call x1, Pallas kernels, shards(): pl.pallas_call(functools.partial(kernel, groups, copies, scale), out_shap...  49 us

profile of v4, /device:TPU:0, one launch (start us, length us, event | category | flops | bytes accessed | tf_op | source)
XLA Modules:
  0.0 130.8 jit_solution(15185758413550340688)
XLA Ops:
  0.6 49.0 %shard_map.110 = (bf16[1,8,16,16,256]{4,3,2,1,0:T(8,128)(2,1)}, bf16[1,8,16,16,256]{4,3,2,1,0:T(8,128)(2,1)}, f32[2,256,256]{2,1,0:T(8,128)}, f32[9,2,256]{2,1,0:T(2,128)}, f32[2,256]{1,0:T(2,128)}) custom-call(bf16[1,8,16,16,256]{4,3,2,1,0:T(8,128)(2,1)} %states.1, bf16[1,8,16,16,256]{4,3,2,1,0:T(8,128)(2,1)} %cotangent.1, s32[8,64]{1,0:T(8,128)} %bitcast.5, ...), custom_call_target="tpu_custom_call" | custom-call | tf_op jit(solution)/shard_map/pallas_call | solution.py:608
  49.6 81.2 %shard_map.111 = (bf16[1,8,16,16,256]{4,3,2,1,0:T(8,128)(2,1)}, bf16[1,8,16,16,256]{4,3,2,1,0:T(8,128)(2,1)}, f32[2,256,256]{2,1,0:T(8,128)}, f32[9,2,256]{2,1,0:T(2,128)}, f32[2,256]{1,0:T(2,128)}) custom-call(bf16[1,8,16,16,256]{4,3,2,1,0:T(8,128)(2,1)} %get-tuple-element.15.refs_0_, bf16[1,8,16,16,256]{4,3,2,1,0:T(8,128)(2,1)} %get-tuple-element.16.refs_1_, ...), custom_call_target="tpu_custom_call" | custom-call | tf_op jit(solution)/shard_map/pallas_call | solution.py:655

commit v5 on v4

--- a/solution.py
+++ b/solution.py
@@ -283,6 +283,140 @@
 
     lax.fori_loop(0, groups, send_rows, 0)
 
+    turn = one_hot(
+        iota((line, line), 1)
+        == lax.rem(iota((line, line), 0), tiles) * side + lax.div(iota((line, line), 0), tiles)
+    )
+    turn_back = one_hot(
+        iota((line, line), 1)
+        == lax.rem(iota((line, line), 0), side) * tiles + lax.div(iota((line, line), 0), side)
+    )
+
+    for x in range(4):
+        inbox[x, me] = jnp.zeros((mail, channels), BF16)
+    step = max(s for s in (1, 2, 4) if side % s == 0)
+    chunk = step * line
+
+    def take_states(c, _):
+        for r in range(step):
+            x = states[0, :, c * step + r].reshape(line, channels)
+            pad_in[c * step + r + 1, 1 : side + 1] = dot(turn, x).reshape(side, tiles, channels)
+        return 0
+
+    lax.fori_loop(0, side // step, take_states, 0)
+
+    def take_rims(pad):
+        inner = slice(1, side + 1)
+        for e, piece in enumerate(
+            (pad[1, inner], pad[inner, side], pad[side, inner], pad[inner, 1])
+        ):
+            rims[e * line : (e + 1) * line, :] = piece.reshape(line, channels).astype(BF16)
+
+    def post_rims(x, pad):
+        take_rims(pad)
+        out = dot(send_map[...], rims[...])
+        outbox[x] = out.astype(BF16).reshape(groups, mail, channels)
+        send(x)
+
+    def fill_halo(x, pad):
+        panels = dot(fetch_map[:, :edge], rims[...]) + dot(
+            fetch_map[:, edge:], inbox[x].reshape(groups * mail, channels)
+        )
+        inner = slice(1, side + 1)
+        strip = lambda d: panels[d * line : (d + 1) * line].reshape(side, tiles, channels)
+        pad[0, inner] = strip(0)
+        pad[inner, side + 1] = strip(1)
+        pad[side + 1, inner] = strip(2)
+        pad[inner, 0] = strip(3)
+        spot = lambda d: panels[edge + d * tiles : edge + (d + 1) * tiles]
+        pad[0, side + 1] = spot(0)
+        pad[side + 1, side + 1] = spot(1)
+        pad[side + 1, 0] = spot(2)
+        pad[0, 0] = spot(3)
+
+    halves = [slice(h, min(h + 128, channels)) for h in range(0, channels, 128)]
+
+    def convolve(pad, layer):
+        def body(y, _):
+            pieces = []
+            for half in halves:
+                total = None
+                for a in range(3):
+                    for b in range(3):
+                        tap = stencils[3 * a + b, layer : layer + 1, half]
+                        term = tap[None] * pad[y + a, b : b + side, :, half]
+                        total = term if total is None else total + term
+                pieces.append(total.reshape(line, total.shape[2]).astype(BF16))
+            conv[pl.ds(pl.multiple_of(y * line, line), line), :] = jnp.concatenate(pieces, axis=1)
+            return 0
+
+        lax.fori_loop(0, side, body, 0)
+
+    def convolve_back(wide, out, layer):
+        def body(y, _):
+            for half in halves:
+                total = None
+                for a in range(3):
+                    for b in range(3):
+                        tap = stencils[3 * a + b, layer : layer + 1, half]
+                        term = tap[None] * wide[y + 2 - a, 2 - b : 2 - b + side + 2, :, half]
+                        total = term if total is None else total + term
+                out[y, :, :, half] = total
+            return 0
+
+        lax.fori_loop(0, side + 2, body, 0)
+
+    extra = 2 * channels
+
+    def stencil_sums(wide, pad, layer):
+        for half in halves:
+
+            def body(y, held):
+                grad = wide[y + 2, 2 : side + 2, :, half]
+                new = []
+                for a in range(3):
+                    for b in range(3):
+                        term = jnp.sum(grad * pad[y + a, b : b + side, :, half], axis=0)
+                        new.append(held[3 * a + b] + term)
+                return tuple(new)
+
+            held = lax.fori_loop(
+                0, side, body, tuple(jnp.zeros((tiles, 128), F32) for _ in range(9))
+            )
+            for tap in range(9):
+                row = extra + 9 * layer + tap
+                sums[row : row + 1, half] = jnp.sum(held[tap], axis=0, keepdims=True) * scale
+
+    def post_parts(x, back):
+        inner = slice(1, side + 1)
+        for d, piece in enumerate(
+            (back[0, inner], back[inner, side + 1], back[side + 1, inner], back[inner, 0])
+        ):
+            parts[d * line : (d + 1) * line, :] = piece.reshape(line, channels).astype(BF16)
+        parts[edge : edge + 4 * tiles, :] = jnp.concatenate(
+            [back[0, side + 1], back[side + 1, side + 1], back[side + 1, 0], back[0, 0]], axis=0
+        ).astype(BF16)
+        out = dot(fetch_map[:, edge:], parts[...], 0, 0)
+        outbox[x] = out.astype(BF16).reshape(groups, mail, channels)
+        send(x)
+
+    def add_rims(back, grads):
+        inner = slice(1, side + 1)
+        strip = lambda e: grads[e * line : (e + 1) * line].reshape(side, tiles, channels)
+        back[1, inner] = back[1, inner] + strip(0)
+        back[inner, side] = back[inner, side] + strip(1)
+        back[side, inner] = back[side, inner] + strip(2)
+        back[inner, 1] = back[inner, 1] + strip(3)
+
+    def add_local(back):
+        add_rims(back, dot(fetch_map[:, :edge], parts[...], 0, 0))
+
+    def add_remote(x, back):
+        add_rims(back, dot(send_map[...], inbox[x].reshape(groups * mail, channels), 0, 0))
+
+    pl.semaphore_wait(barrier, groups + copies - 2)
+    post_rims(0, pad_in)
+
     owner, base, flip, place = block_columns(me)
     remote = owner != me
     base = jnp.where(remote, edge + (owner * CAP + place) * side, base)
@@ -305,144 +439,11 @@
         corner.append(jnp.where(iota((tiles, pool), 1) == want, 1.0, 0.0))
     fetch_map[edge : edge + 4 * tiles, :] = jnp.concatenate(corner, axis=0).astype(BF16)
 
-    turn = one_hot(
-        iota((line, line), 1)
-        == lax.rem(iota((line, line), 0), tiles) * side + lax.div(iota((line, line), 0), tiles)
-    )
-    turn_back = one_hot(
-        iota((line, line), 1)
-        == lax.rem(iota((line, line), 0), side) * tiles + lax.div(iota((line, line), 0), side)
-    )
-
-    for x in range(4):
-        inbox[x, me] = jnp.zeros((mail, channels), BF16)
     for wide in (wide_second, wide_first):
         for rows in (slice(0, 2), slice(side + 2, side + 4)):
             wide[rows] = jnp.zeros((2, side + 4, tiles, channels), F32)
             wide[2 : side + 2, rows] = jnp.zeros((side, 2, tiles, channels), F32)
 
-    step = max(s for s in (1, 2, 4) if side % s == 0)
-    chunk = step * line
-
-    def take_states(c, _):
-        for r in range(step):
-            x = states[0, :, c * step + r].reshape(line, channels)
-            pad_in[c * step + r + 1, 1 : side + 1] = dot(turn, x).reshape(side, tiles, channels)
-        return 0
-
-    lax.fori_loop(0, side // step, take_states, 0)
-
-    def take_rims(pad):
-        inner = slice(1, side + 1)
-        for e, piece in enumerate(
-            (pad[1, inner], pad[inner, side], pad[side, inner], pad[inner, 1])
-        ):
-            rims[e * line : (e + 1) * line, :] = piece.reshape(line, channels).astype(BF16)
-
-    def post_rims(x, pad):
-        take_rims(pad)
-        out = dot(send_map[...], rims[...])
-        outbox[x] = out.astype(BF16).reshape(groups, mail, channels)
-        send(x)
-
-    def fill_halo(x, pad):
-        panels = dot(fetch_map[:, :edge], rims[...]) + dot(
-            fetch_map[:, edge:], inbox[x].reshape(groups * mail, channels)
-        )
-        inner = slice(1, side + 1)
-        strip = lambda d: panels[d * line : (d + 1) * line].reshape(side, tiles, channels)
-        pad[0, inner] = strip(0)
-        pad[inner, side + 1] = strip(1)
-        pad[side + 1, inner] = strip(2)
-        pad[inner, 0] = strip(3)
-        spot = lambda d: panels[edge + d * tiles : edge + (d + 1) * tiles]
-        pad[0, side + 1] = spot(0)
-        pad[side + 1, side + 1] = spot(1)
-        pad[side + 1, 0] = spot(2)
-        pad[0, 0] = spot(3)
-
-    halves = [slice(h, min(h + 128, channels)) for h in range(0, channels, 128)]
-
-    def convolve(pad, layer):
-        def body(y, _):
-            pieces = []
-            for half in halves:
-                total = None
-                for a in range(3):
-                    for b in range(3):
-                        tap = stencils[3 * a + b, layer : layer + 1, half]
-                        term = tap[None] * pad[y + a, b : b + side, :, half]
-                        total = term if total is None else total + term
-                pieces.append(total.reshape(line, total.shape[2]).astype(BF16))
-            conv[pl.ds(pl.multiple_of(y * line, line), line), :] = jnp.concatenate(pieces, axis=1)
-            return 0
-
-        lax.fori_loop(0, side, body, 0)
-
-    def convolve_back(wide, out, layer):
-        def body(y, _):
-            for half in halves:
-                total = None
-                for a in range(3):
-                    for b in range(3):
-                        tap = stencils[3 * a + b, layer : layer + 1, half]
-                        term = tap[None] * wide[y + 2 - a, 2 - b : 2 - b + side + 2, :, half]
-                        total = term if total is None else total + term
-                out[y, :, :, half] = total
-            return 0
-
-        lax.fori_loop(0, side + 2, body, 0)
-
-    extra = 2 * channels
-
-    def stencil_sums(wide, pad, layer):
-        for half in halves:
-
-            def body(y, held):
-                grad = wide[y + 2, 2 : side + 2, :, half]
-                new = []
-                for a in range(3):
-                    for b in range(3):
-                        term = jnp.sum(grad * pad[y + a, b : b + side, :, half], axis=0)
-                        new.append(held[3 * a + b] + term)
-                return tuple(new)
-
-            held = lax.fori_loop(
-                0, side, body, tuple(jnp.zeros((tiles, 128), F32) for _ in range(9))
-            )
-            for tap in range(9):
-                row = extra + 9 * layer + tap
-                sums[row : row + 1, half] = jnp.sum(held[tap], axis=0, keepdims=True) * scale
-
-    def post_parts(x, back):
-        inner = slice(1, side + 1)
-        for d, piece in enumerate(
-            (back[0, inner], back[inner, side + 1], back[side + 1, inner], back[inner, 0])
-        ):
-            parts[d * line : (d + 1) * line, :] = piece.reshape(line, channels).astype(BF16)
-        parts[edge : edge + 4 * tiles, :] = jnp.concatenate(
-            [back[0, side + 1], back[side + 1, side + 1], back[side + 1, 0], back[0, 0]], axis=0
-        ).astype(BF16)
-        out = dot(fetch_map[:, edge:], parts[...], 0, 0)
-        outbox[x] = out.astype(BF16).reshape(groups, mail, channels)
-        send(x)
-
-    def add_rims(back, grads):
-        inner = slice(1, side + 1)
-        strip = lambda e: grads[e * line : (e + 1) * line].reshape(side, tiles, channels)
-        back[1, inner] = back[1, inner] + strip(0)
-        back[inner, side] = back[inner, side] + strip(1)
-        back[side, inner] = back[side, inner] + strip(2)
-        back[inner, 1] = back[inner, 1] + strip(3)
-
-    def add_local(back):
-        add_rims(back, dot(fetch_map[:, :edge], parts[...], 0, 0))
-
-    def add_remote(x, back):
-        add_rims(back, dot(send_map[...], inbox[x].reshape(groups * mail, channels), 0, 0))
-
-    pl.semaphore_wait(barrier, groups + copies - 2)
-    post_rims(0, pad_in)
 
     shares[2][...] = jnp.zeros(shares[2].shape, F32)
 
@@ -576,12 +577,17 @@
 
 
 def hand_on(*refs):
-    sources, targets, sems = refs[:5], refs[5:10], refs[10]
-    moves = [pltpu.make_async_copy(sources[k], targets[k], sems.at[k]) for k in range(5)]
-    for move in moves:
-        move.start()
-    for move in moves:
-        move.wait()
+    sources, targets, held = refs[:5], refs[5:10], refs[10:15]
+    into, out = refs[15], refs[16]
+    reads = [pltpu.make_async_copy(sources[k], held[k], into.at[k]) for k in range(5)]
+    writes = [pltpu.make_async_copy(held[k], targets[k], out.at[k]) for k in range(5)]
+    for read in reads:
+        read.start()
+    for read, write in zip(reads, writes):
+        read.wait()
+        write.start()
+    for write in writes:
+        write.wait()
 
 
 def shards(states, cotangent, beside_slot, beside_code, mixers, stencils, shifts):
@@ -657,7 +663,11 @@
         out_shape=[jax.ShapeDtypeStruct(r.shape, r.dtype) for r in results],
         in_specs=[anywhere] * 5,
         out_specs=[anywhere] * 5,
-        scratch_shapes=[pltpu.SemaphoreType.DMA((5,))],
+        scratch_shapes=[
+            *[pltpu.VMEM(r.shape, r.dtype) for r in results],
+            pltpu.SemaphoreType.DMA((5,)),
+            pltpu.SemaphoreType.DMA((5,)),
+        ],
         compiler_params=pltpu.CompilerParams(vmem_limit_bytes=56 * 1024 * 1024),
     )(*results)
     return (outcome, state_grad, mixer_grads, stencil_grads.transpose(1, 0, 2), shift_grads)

time: 131 us -> 52.6 us (0.40)
  Pallas kernels: 130 us -> 51.8 us
    pallas_call x1, Pallas kernels: 81.2 us -> 2.8 us  [shards(): pl.pallas_call(hand_on, out_shape=[jax.ShapeDtypeStruct(r.shape, r.dtype)...]
where the time goes in v5:
time: 52.6 us; the launch traced here: 52.4 us
  Pallas kernels  51.8 us (98%)
  between operations  0.64 us (1%)
    pallas_call x1, Pallas kernels, shards(): pl.pallas_call(functools.partial(kernel, groups, copies, scale), out_shap...  49 us
    pallas_call x1, Pallas kernels, shards(): pl.pallas_call(hand_on, out_shape=[jax.ShapeDtypeStruct(r.shape, r.dtype)...  2.8 us

profile of v5, /device:TPU:0, one launch (start us, length us, event | category | flops | bytes accessed | tf_op | source)
XLA Modules:
  0.0 52.4 jit_solution(11912612347062604588)
XLA Ops:
  0.6 49.0 %shard_map.110 = (bf16[1,8,16,16,256]{4,3,2,1,0:T(8,128)(2,1)}, bf16[1,8,16,16,256]{4,3,2,1,0:T(8,128)(2,1)}, f32[2,256,256]{2,1,0:T(8,128)}, f32[9,2,256]{2,1,0:T(2,128)}, f32[2,256]{1,0:T(2,128)}) custom-call(bf16[1,8,16,16,256]{4,3,2,1,0:T(8,128)(2,1)} %states.1, bf16[1,8,16,16,256]{4,3,2,1,0:T(8,128)(2,1)} %cotangent.1, s32[8,64]{1,0:T(8,128)} %bitcast.5, ...), custom_call_target="tpu_custom_call" | custom-call | tf_op jit(solution)/shard_map/pallas_call | solution.py:614
  49.6 2.8 %shard_map.111 = (bf16[1,8,16,16,256]{4,3,2,1,0:T(8,128)(2,1)}, bf16[1,8,16,16,256]{4,3,2,1,0:T(8,128)(2,1)}, f32[2,256,256]{2,1,0:T(8,128)}, f32[9,2,256]{2,1,0:T(2,128)}, f32[2,256]{1,0:T(2,128)}) custom-call(bf16[1,8,16,16,256]{4,3,2,1,0:T(8,128)(2,1)} %get-tuple-element.15.refs_0_, bf16[1,8,16,16,256]{4,3,2,1,0:T(8,128)(2,1)} %get-tuple-element.16.refs_1_, ...), custom_call_target="tpu_custom_call" | custom-call | tf_op jit(solution)/shard_map/pallas_call | solution.py:661
